TPU v7x, 32 devices: a whole 2x2x4 slice. The times are simulated.
32 devices in a mesh: pair: 8 (over y, x, core), slab: 4 (over z).
Axes of the slice: x: 2, y: 2, z: 4, core: 2. Of those that a mesh axis runs over, the one named last changes fastest.
Arguments:
- amplitudes: bfloat16 [8, 8, 160000], P('pair'), may hold values from -6 to 6
- integrals: bfloat16 [160000, 1024], P('pair', 'slab'), may hold values from -0.0390625 to 0.0390625
- virt_irrep: int32 [400], replicated, may hold values from 0 to 7
- occ_energy: float32 [8], replicated, may hold values from -1.2 to -0.3
- slab_energy: float32 [32], replicated, may hold values from 0.1 to 1.5
Outputs:
- update: float32 [8, 8, 32, 32], P('pair', None, 'slab')
All inputs are finite; a program needn't handle non-finite values.
Results may differ from a plain program's by a relative error of at most 0.0003.
Values may be sent and summed in bfloat16 or wider, within the bound.
No kernel may reach another device: no remote copies, remote signals or barrier semaphores. Data moves between devices by JAX's collectives and lax.ppermute only.
A program may use at most 256 MiB of HBM per device.

v0:
```python
import functools
import math

import jax
import jax.numpy as jnp
from jax import lax
from jax.experimental import pallas as pl
from jax.experimental.pallas import tpu as pltpu
from jax.sharding import PartitionSpec as P

IRREPS = 8
MIB = 2**20
SHARE = 0.25
TIE_FLOPS = 10**10


def start_of(part, slab_ref, shared):
    parity = slab_ref[0] % 2
    return pl.multiple_of({"own": parity * shared, "other": (1 - parity) * shared, "rest": 2 * shared, "all": 0}[part], 128)


def pack_kernel(rows_local, shared, which, me_ref, slab_ref, amps_ref, other_ref, after_ref, *refs):
    outs, (held, packed, sems) = refs[:-3], refs[-3:]
    size = packed.shape[-1]
    count = sems.shape[0]
    me = me_ref[0]
    start = start_of(which, slab_ref, shared)
    sources = [amps_ref] if which == "own" else [amps_ref, other_ref]
    wanted = {
        "own": lambda dest: (dest ^ me) >= 2,
        "rest": lambda dest: jnp.logical_and(((dest ^ me) & 1) == 0, dest != me),
        "all": lambda dest: dest == me,
    }[which]
    slots = {"own": lambda dest: dest, "rest": lambda dest: dest // 2, "all": lambda dest: 0}[which]

    def load(dest, source):
        first = dest * rows_local // 128 * 128
        width = -(-(dest * rows_local - first + size) // 128) * 128
        return pltpu.make_async_copy(
            sources[source].at[:, pl.ds(start + first, width)],
            held.at[slots(dest), source, :, pl.ds(0, width)],
            sems.at[dest, source],
        )

    for dest in range(count):

        @pl.when(wanted(dest))
        def _():
            for source in range(len(sources)):
                load(dest, source).start()

    for dest in range(count):

        @pl.when(wanted(dest))
        def _():
            shift = dest * rows_local % 128
            for source in range(len(sources)):
                load(dest, source).wait()
                block = held[slots(dest), source, :, shift : shift + size]
                if which == "own":
                    packed[dest ^ me] = block
                elif which == "rest":
                    packed[(dest ^ me) // 2, source] = block
                else:
                    outs[0][source] = block

    if which == "own":
        for k, out in enumerate(outs):
            out[...] = packed[2 * k + 2 : 2 * k + 4]
    elif which == "rest":
        for k, out in enumerate(outs):
            out[...] = packed[k + 1]


def pack(amps, other, me, slab, shared, which, pair_count, after):
    rows, virt_pairs = amps.shape
    rows_local = virt_pairs // pair_count
    size = {"own": shared, "rest": rows_local - 2 * shared, "all": rows_local}[which]
    slots = {"own": pair_count, "rest": pair_count // 2, "all": 1}[which]
    sources = 1 if which == "own" else 2
    held = (slots, sources, rows, -(-size // 128) * 128 + 128)
    packed = {"own": (pair_count, rows, size), "rest": (pair_count // 2, 2, rows, size), "all": (1, rows, size)}[which]
    outs = 1 if which == "all" else pair_count // 2 - 1
    return pl.pallas_call(
        functools.partial(pack_kernel, rows_local, shared, which),
        out_shape=[jax.ShapeDtypeStruct((2, rows, size), amps.dtype)] * outs,
        in_specs=[pl.BlockSpec(memory_space=pltpu.SMEM)] * 2 + [pl.BlockSpec(memory_space=pl.ANY)] * 3,
        out_specs=[pl.BlockSpec(memory_space=pltpu.VMEM)] * outs,
        scratch_shapes=[
            pltpu.VMEM(held, amps.dtype),
            pltpu.VMEM(packed, amps.dtype),
            pltpu.SemaphoreType.DMA((pair_count, sources)),
        ],
        compiler_params=pltpu.CompilerParams(vmem_limit_bytes=2 * MIB + 6 * slots * sources * rows * held[3]),
        cost_estimate=pl.CostEstimate(
            flops=0, bytes_accessed=4 * slots * sources * rows * size, transcendentals=0
        ),
        name="pack_" + which,
    )(me, slab, pltpu.with_memory_space_constraint(amps, pltpu.HBM), other, after)


def mask_kernel(per_step, parts, me_ref, slab_ref, irrep_ref, occ_ref, virt_ref, row_ref, ints_ref, *refs):
    _, out_ref, by_slab_ref, by_first_ref, denominator_ref, table, padded, by_row = refs
    step = pl.program_id(0)
    chunk, cols = ints_ref.shape[1:]
    slab_virt = virt_ref.shape[0]
    first_local = cols // slab_virt
    bits = slab_virt.bit_length() - 1
    me, slab = me_ref[0], slab_ref[0]

    @pl.when(step == 0)
    def _():
        padded[:, : row_ref.shape[1]] = row_ref[...]
        for k in range(padded.shape[1] // 128):
            lanes = slice(k * 128, (k + 1) * 128)
            by_row[lanes] = jnp.transpose(jnp.broadcast_to(padded[:, lanes], (128, 128)))

        col = lax.broadcasted_iota(jnp.int32, (1, cols), 1)
        a_of, b_of = col >> bits, col & (slab_virt - 1)
        irrep_a = irrep_b = jnp.zeros_like(col)
        energy_a = energy_b = jnp.zeros(col.shape, jnp.float32)
        for a in range(first_local):
            irrep_a = jnp.where(a_of == a, irrep_ref[slab * first_local + a], irrep_a)
            energy_a = jnp.where(a_of == a, virt_ref[slab * first_local + a], energy_a)
        for b in range(slab_virt):
            irrep_b = jnp.where(b_of == b, irrep_ref[b], irrep_b)
            energy_b = jnp.where(b_of == b, virt_ref[b], energy_b)
        irrep_ab = irrep_a ^ irrep_b

        for part in range(parts):
            for lanes in (slice(k, k + 128) for k in range(0, cols, 128)):
                needed = by_row[part * chunk : (part + 1) * chunk] ^ irrep_ab[:, lanes]
                for irrep in range(IRREPS):
                    table[irrep * parts + part, :, lanes] = jnp.where(needed == irrep, 1.0, 0.0).astype(table.dtype)

        occupied = denominator_ref.shape[0]
        j_of = lax.broadcasted_iota(jnp.int32, (occupied, cols), 0)
        energy_j = jnp.zeros((occupied, cols), jnp.float32)
        for j in range(occupied):
            energy_j = jnp.where(j_of == j, occ_ref[j], energy_j)
        denominator_ref[...] = energy_a + energy_b - occ_ref[me] - energy_j

        row = lax.broadcasted_iota(jnp.int32, (cols, cols), 0)
        col = lax.broadcasted_iota(jnp.int32, (cols, cols), 1)
        first_bits = first_local.bit_length() - 1
        low = first_local - 1
        slabs = slab_virt // first_local
        source = (((col >> first_bits) & low) << bits) + ((col >> (2 * first_bits)) << first_bits) + (col & low)
        by_slab_ref[...] = jnp.where(row == source, 1.0, 0.0).astype(by_slab_ref.dtype)
        source = (((col >> first_bits) & (slabs - 1)) << (2 * first_bits)) + ((col & low) << first_bits) + (col >> bits)
        by_first_ref[...] = jnp.where(row == source, 1.0, 0.0).astype(by_first_ref.dtype)

    chunks = per_step * pl.num_programs(0)
    for k in range(per_step):
        index = me * chunks + step * per_step + k
        irrep_c = irrep_ref[index // parts]
        out_ref[k] = ints_ref[k] * table[irrep_c * parts + index % parts]


def in_hbm(array):
    return pltpu.with_memory_space_constraint(array, pltpu.HBM)


def mask(integrals, me, slab, virt_irrep, occ_energy, slab_energy, after):
    virtuals = virt_irrep.shape[0]
    slab_virt = slab_energy.shape[0]
    occupied = occ_energy.shape[0]
    rows_local, cols_local = integrals.shape
    chunk = math.gcd(virtuals, rows_local)
    parts = virtuals // chunk
    chunks = rows_local // chunk
    per_step = next(n for n in (10, 5, 4, 2, 1) if chunks % n == 0)
    padded = -(-virtuals // 128) * 128
    square = jax.ShapeDtypeStruct((cols_local, cols_local), jnp.bfloat16)
    block = pl.BlockSpec((per_step, chunk, cols_local), lambda step: (step, 0, 0))
    scalars = pl.BlockSpec(memory_space=pltpu.SMEM)
    masked, by_slab, by_first, denominator = pl.pallas_call(
        functools.partial(mask_kernel, per_step, parts),
        grid=(chunks // per_step,),
        in_specs=[scalars] * 5
        + [pl.BlockSpec((1, virtuals), lambda step: (0, 0)), block, pl.BlockSpec(memory_space=pl.ANY)],
        out_specs=[
            block,
            pl.BlockSpec(square.shape, lambda step: (0, 0)),
            pl.BlockSpec(square.shape, lambda step: (0, 0)),
            pl.BlockSpec((occupied, cols_local), lambda step: (0, 0)),
        ],
        scratch_shapes=[
            pltpu.VMEM((IRREPS * parts, chunk, cols_local), integrals.dtype),
            pltpu.VMEM((1, padded), jnp.int32),
            pltpu.VMEM((padded, 128), jnp.int32),
        ],
        out_shape=[
            pltpu.VMEM((chunks, chunk, cols_local), integrals.dtype),
            square,
            square,
            jax.ShapeDtypeStruct((occupied, cols_local), jnp.float32),
        ],
        compiler_params=pltpu.CompilerParams(vmem_limit_bytes=16 * MIB),
        cost_estimate=pl.CostEstimate(
            flops=0, bytes_accessed=0, transcendentals=0
        ),
        name="mask_integrals",
    )(
        me,
        slab,
        *(in_hbm(array) for array in (virt_irrep, occ_energy, slab_energy, virt_irrep.reshape(1, virtuals))),
        in_hbm(integrals.reshape(chunks, chunk, cols_local)),
        after,
    )
    return masked.reshape(rows_local, cols_local), by_slab, by_first, denominator


def take_kernel(*refs):
    parts, out_ref = refs[:-2], refs[-1]
    for k, part in enumerate(parts):
        out_ref[k] = part[1]


def take_other(parts, after):
    count = len(parts)
    _, rows, size = parts[0].shape
    vmem = pl.BlockSpec(memory_space=pltpu.VMEM)
    return pl.pallas_call(
        take_kernel,
        out_shape=jax.ShapeDtypeStruct((count, rows, size), parts[0].dtype),
        in_specs=[vmem] * count + [pl.BlockSpec(memory_space=pl.ANY)],
        out_specs=vmem,
        compiler_params=pltpu.CompilerParams(vmem_limit_bytes=4 * MIB),
        cost_estimate=pl.CostEstimate(flops=0, bytes_accessed=4 * count * rows * size, transcendentals=0),
        name="take_other",
    )(*parts, after)


def join_kernel(*refs):
    parts, other_ref, out_ref = refs[:-2], refs[-2], refs[-1]
    for k, part in enumerate(parts):
        out_ref[k, 0] = part[0]
        out_ref[k, 1] = other_ref[k]


def join(parts, other):
    vmem = pl.BlockSpec(memory_space=pltpu.VMEM)
    return pl.pallas_call(
        join_kernel,
        out_shape=jax.ShapeDtypeStruct((len(parts),) + parts[0].shape, other.dtype),
        in_specs=[vmem] * (len(parts) + 1),
        out_specs=vmem,
        compiler_params=pltpu.CompilerParams(vmem_limit_bytes=4 * MIB),
        cost_estimate=pl.CostEstimate(flops=0, bytes_accessed=8 * other.size, transcendentals=0),
        name="join",
    )(*parts, other)


def tie_kernel(*refs):
    del refs


def tie(parts, after, flops=0):
    count = len(parts)
    anywhere = pl.BlockSpec(memory_space=pl.ANY)
    return pl.pallas_call(
        tie_kernel,
        out_shape=[pltpu.VMEM(part.shape, part.dtype) for part in parts],
        in_specs=[anywhere] * (count + 1),
        out_specs=[anywhere] * count,
        input_output_aliases={k: k for k in range(count)},
        compiler_params=pltpu.CompilerParams(vmem_limit_bytes=2 * MIB),
        cost_estimate=pl.CostEstimate(flops=flops, bytes_accessed=0, transcendentals=0),
        name="tie",
    )(*(pltpu.with_memory_space_constraint(part, pltpu.VMEM) for part in parts), after)


def select_exactly(values, select):
    rows = values.shape[0]
    high = values.astype(jnp.bfloat16)
    rest = values - high.astype(jnp.float32)
    middle = rest.astype(jnp.bfloat16)
    low = (rest - middle.astype(jnp.float32)).astype(jnp.bfloat16)
    terms = [jnp.dot(term, select, preferred_element_type=jnp.float32) for term in (high, middle, low)]
    return terms[0] + terms[1] + terms[2]


def contract_kernel(which, shared, slab_ref, me_ref, home_ref, ints_ref, *refs):
    last = which == "other"
    lhs = refs[-2] if last else refs[-1]
    count, rows, size = lhs.shape
    chips = count // 2 - 1
    start = start_of(which, slab_ref, shared)
    lhs[:2] = home_ref[:, :, pl.ds(start, size)]
    for k in range(chips):
        if which == "rest":
            lhs[2 * k + 2 : 2 * k + 4] = refs[k][...]
        else:
            lhs[2 * k + 2 : 2 * k + 4] = refs[0][k]
    refs = refs[chips if which == "rest" else 1 :]
    step = 2560
    total = None
    for first in range(0, size, step):
        width = min(step, size - first)
        block = lhs[:, :, first : first + width].reshape(count * rows, width)
        part = jnp.dot(block, ints_ref[pl.ds(start + first, width)], preferred_element_type=jnp.float32)
        total = part if total is None else total + part
    if not last:
        before, out_ref = refs[:-2], refs[-2]
        out_ref[...] = total + before[0][...] if before else total
        return
    before_ref, own_ref, other_ref, total_ref, _, partial = refs
    total = total + before_ref[...]
    total_ref[...] = total
    partial[...] = total.reshape(partial.shape)
    for k in range(count // 2):
        own_ref[k] = partial[2 * k]
        other_ref[k] = partial[2 * k + 1]


def mirror_kernel(me_ref, total_ref, select_ref, out_ref, chosen, ordered):
    count = chosen.shape[0]
    chosen[...] = select_exactly(total_ref[...], select_ref[...]).reshape(chosen.shape)
    for i in range(count):
        ordered[i] = chosen[i ^ me_ref[0]]
    slabs = out_ref.shape[0] // count
    half, width = out_ref.shape[1], out_ref.shape[2] // 2
    for p in range(count):
        block = ordered[:, p, :]
        for s in range(slabs):
            part = block[:, s * width : (s + 1) * width]
            out_ref[p * slabs + s, :, :width] = part[:half]
            out_ref[p * slabs + s, :, width:] = part[half:]


def mirror_blocks(total, select, me, slab_count):
    cols = total.shape[1]
    count = math.isqrt(total.shape[0])
    vmem = pl.BlockSpec(memory_space=pltpu.VMEM)
    return pl.pallas_call(
        mirror_kernel,
        out_shape=jax.ShapeDtypeStruct((count * slab_count, count // 2, 2 * cols // slab_count), jnp.float32),
        in_specs=[pl.BlockSpec(memory_space=pltpu.SMEM), vmem, vmem],
        out_specs=vmem,
        scratch_shapes=[pltpu.VMEM((count, count, cols), jnp.float32)] * 2,
        compiler_params=pltpu.CompilerParams(vmem_limit_bytes=4 * MIB + 40 * total.size),
        cost_estimate=pl.CostEstimate(flops=6 * total.size * cols, bytes_accessed=8 * total.size, transcendentals=0),
        name="mirror_blocks",
    )(me, total, select)


def contract(amps, home, ints, me, slab, shared, which, before=None):
    occupied, size = amps[0].shape[-2:]
    cols = ints.shape[1]
    vmem = pl.BlockSpec(memory_space=pltpu.VMEM)
    operands = [*amps] + ([] if before is None else [before])
    scratch = [pltpu.VMEM((occupied, occupied, size), home.dtype)]
    if which == "other":
        out_shape = [jax.ShapeDtypeStruct((occupied // 2, occupied, cols), jnp.float32)] * 2
        out_shape.append(jax.ShapeDtypeStruct((occupied * occupied, cols), jnp.float32))
        scratch.append(pltpu.VMEM((occupied, occupied, cols), jnp.float32))
    else:
        out_shape = [jax.ShapeDtypeStruct((occupied * occupied, cols), jnp.float32)]
    return pl.pallas_call(
        functools.partial(contract_kernel, which, shared),
        out_shape=out_shape,
        in_specs=[pl.BlockSpec(memory_space=pltpu.SMEM)] * 2 + [vmem] * (2 + len(operands)),
        out_specs=[vmem] * len(out_shape),
        scratch_shapes=scratch,
        compiler_params=pltpu.CompilerParams(
            vmem_limit_bytes=4 * MIB + 40 * occupied * occupied * cols + 4 * occupied * occupied * size
        ),
        cost_estimate=pl.CostEstimate(
            flops=2 * occupied * occupied * size * cols,
            bytes_accessed=2 * size * (cols + occupied * occupied),
            transcendentals=0,
        ),
        name="contract",
    )(slab, me, home, pltpu.with_memory_space_constraint(ints, pltpu.VMEM), *operands)


def add_cores_kernel(mine_ref, other_ref, *outs):
    for k, out in enumerate(outs):
        out[...] = mine_ref[k] + other_ref[k]


def add_cores(mine, other):
    count, rows, cols = mine.shape
    vmem = pl.BlockSpec(memory_space=pltpu.VMEM)
    return pl.pallas_call(
        add_cores_kernel,
        out_shape=[jax.ShapeDtypeStruct((rows, cols), jnp.float32)] * count,
        in_specs=[vmem, vmem],
        out_specs=[vmem] * count,
        compiler_params=pltpu.CompilerParams(vmem_limit_bytes=4 * MIB),
        cost_estimate=pl.CostEstimate(flops=mine.size, bytes_accessed=12 * mine.size, transcendentals=0),
        name="add_cores",
    )(mine, other)


def finish_kernel(mirror_ref, denominator_ref, select_ref, *refs):
    parts, out_ref = refs[:-1], refs[-1]
    ladder = parts[0][...]
    for part in parts[1:]:
        ladder = ladder + part[...]
    _, first_local, slab_virt = out_ref.shape
    slab_count = slab_virt // first_local
    width = mirror_ref.shape[2] // 2
    blocks = []
    for s in range(slab_count):
        block = mirror_ref[s]
        for q in range(1, mirror_ref.shape[0] // slab_count):
            block = block + mirror_ref[q * slab_count + s]
        blocks += [jnp.concatenate([block[:, :width], block[:, width:]], axis=0)]
    mirror = select_exactly(jnp.concatenate(blocks, axis=1), select_ref[...])
    update = (ladder + mirror) / denominator_ref[...]
    for a in range(first_local):
        out_ref[:, a, :] = update[:, a * slab_virt : (a + 1) * slab_virt]


def finish(parts, mirror, denominator, select, first_local, slab_virt):
    rows = parts[0].shape[0]
    return pl.pallas_call(
        finish_kernel,
        out_shape=jax.ShapeDtypeStruct((rows, first_local, slab_virt), jnp.float32),
        in_specs=[pl.BlockSpec(memory_space=pltpu.VMEM)] * (3 + len(parts)),
        out_specs=pl.BlockSpec(memory_space=pltpu.VMEM),
        compiler_params=pltpu.CompilerParams(vmem_limit_bytes=6 * MIB),
        cost_estimate=pl.CostEstimate(flops=6 * rows * select.size, bytes_accessed=2 * select.size, transcendentals=0),
        name="finish",
    )(mirror, denominator, select, *parts)


def swap(values, axis, bits):
    return lax.ppermute(values, axis, [(p, p ^ bits) for p in range(lax.axis_size(axis))])


def local(amplitudes, integrals, virt_irrep, occ_energy, slab_energy):
    pair_count = lax.axis_size("pair")
    slab_count = lax.axis_size("slab")
    occ_local, occupied, virt_pairs = amplitudes.shape
    rows_local, cols_local = integrals.shape
    slab_virt = slab_energy.shape[0]
    first_local = slab_virt // slab_count
    assert occ_local == 1
    me = lax.axis_index("pair").astype(jnp.int32).reshape(1)
    slab = lax.axis_index("slab").astype(jnp.int32).reshape(1)

    shared = int(SHARE * rows_local) // 128 * 128
    amps = amplitudes.reshape(occupied, virt_pairs)
    chips = [2 * k for k in range(1, pair_count // 2)]

    def to_chips(parts):
        return [swap(part, "pair", bits) for part, bits in zip(parts, chips)]

    other = swap(amps, "pair", 1)
    parts = pack(amps, me, me, slab, shared, "own", pair_count, me)
    own_amps = to_chips(parts)
    parts = pack(amps, other, me, slab, shared, "rest", pair_count, parts[-1])
    rest_amps = to_chips(parts)
    (home,) = pack(amps, other, me, slab, shared, "all", pair_count, parts[-1])

    own_amps = join(own_amps, swap(take_other(own_amps, home), "pair", 1))
    other_amps = swap(own_amps, "slab", 1)
    masked, by_slab, by_first, denominator = mask(integrals, me, slab, virt_irrep, occ_energy, slab_energy, own_amps)
    rest_amps = tie(rest_amps, denominator, TIE_FLOPS)
    place = (home, masked, me, slab, shared)
    (partial,) = contract([own_amps], *place, "own")
    (partial,) = contract(rest_amps, *place, "rest", partial)
    even, odd, total = contract([other_amps], *place, "other", partial)

    odd = swap(odd, "pair", 1)
    (mirror,) = tie([mirror_blocks(total, by_slab, me, slab_count)], odd)
    mirror = lax.all_to_all(mirror, ("pair", "slab"), split_axis=0, concat_axis=0, tiled=True)
    parts = add_cores(even, odd)
    parts = [parts[0]] + [swap(parts[k], "pair", 2 * k) for k in reversed(range(1, pair_count // 2))]
    update = finish(parts, mirror, denominator, by_first, first_local, slab_virt)
    return update.reshape(occ_local, occupied, first_local, slab_virt)


def solution(mesh):
    placed = (P("pair", None, None), P("pair", "slab"), P(), P(), P())
    return jax.shard_map(
        local, mesh=mesh, in_specs=placed, out_specs=P("pair", None, "slab", None), check_vma=False
    )
```

profile of v0, /device:TPU:0, one launch (start us, length us, event | category | flops | bytes accessed | tf_op | source)
XLA Modules:
  0.0 44.8 jit_solution(16459576596143566293)
XLA Ops:
  0.5 1.4 %pack_own.1 = (bf16[2,8,4992]{2,1,0:T(8,128)(2,1)S(1)}, bf16[2,8,4992]{2,1,0:T(8,128)(2,1)S(1)}, bf16[2,8,4992]{2,1,0:T(8,128)(2,1)S(1)}) custom-call(s32[1]{0:T(128)} %bitcast.me_ref.other_ref.after_ref, s32[1]{0:T(128)} %bitcast.1.slab_ref, bf16[8,160000]{1,0:T(8,128)(2,1)} %bitcast.11, s32[1]{0:T(128)} %bitcast.me_ref.other_ref.after_ref, ...), custom_call_target="tpu_custom_call" | custom-call | bytes 1277952 | tf_op jit(solution)/shard_map/pack_own/pallas_call | solution.py:84
  1.9 2.5 %collective-permute-start.1 = (bf16[2,8,4992]{2,1,0:T(8,128)(2,1)S(1)}, bf16[2,8,4992]{2,1,0:T(8,128)(2,1)S(1)}, u32[]{:S(2)}, u32[]{:S(2)}) collective-permute-start(bf16[2,8,4992]{2,1,0:T(8,128)(2,1)S(1)} %get-tuple-element.27), channel_id=1, source_target_pairs={{0,8},{4,12},{8,0},{12,4},{16,24},{20,28},{24,16},{28,20},{1,9},{5... | collective-permute-start | bytes 479240 | tf_op jit(solution)/shard_map/ppermute | solution.py:431
  4.4 1.5 %collective-permute-start.2 = (bf16[2,8,4992]{2,1,0:T(8,128)(2,1)S(1)}, bf16[2,8,4992]{2,1,0:T(8,128)(2,1)S(1)}, u32[]{:S(2)}, u32[]{:S(2)}) collective-permute-start(bf16[2,8,4992]{2,1,0:T(8,128)(2,1)S(1)} %get-tuple-element.28), channel_id=1, source_target_pairs={{0,16},{4,20},{8,24},{12,28},{16,0},{20,4},{24,8},{28,12},{1,17},{... | collective-permute-start | bytes 479240 | tf_op jit(solution)/shard_map/ppermute | solution.py:431
  6.0 1.8 %pack_rest.1 = (bf16[2,8,10016]{2,1,0:T(8,128)(2,1)S(1)}, bf16[2,8,10016]{2,1,0:T(8,128)(2,1)S(1)}, bf16[2,8,10016]{2,1,0:T(8,128)(2,1)S(1)}) custom-call(s32[1]{0:T(128)} %bitcast.me_ref.other_ref.after_ref, s32[1]{0:T(128)} %bitcast.1.slab_ref, bf16[8,160000]{1,0:T(8,128)(2,1)} %bitcast.12, bf16[8,160000]{1,0:T(8,128)(2,1)S(1)} %collective-permute-done.other_ref, ...), custom_call_target="tpu_custom_call" | custom-call | bytes 2564096 | tf_op jit(solution)/shard_map/pack_rest/pallas_call | solution.py:84
  7.8 2.0 %collective-permute-start.6 = (bf16[2,8,10016]{2,1,0:T(8,128)(2,1)S(1)}, bf16[2,8,10016]{2,1,0:T(8,128)(2,1)S(1)}, u32[]{:S(2)}, u32[]{:S(2)}) collective-permute-start(bf16[2,8,10016]{2,1,0:T(8,128)(2,1)S(1)} %get-tuple-element.30), channel_id=1, source_target_pairs={{0,8},{4,12},{8,0},{12,4},{16,24},{20,28},{24,16},{28,20},{1,9},{5... | collective-permute-start | bytes 961544 | tf_op jit(solution)/shard_map/ppermute | solution.py:431
  9.8 1.3 %collective-permute-start.7 = (bf16[2,8,10016]{2,1,0:T(8,128)(2,1)S(1)}, bf16[2,8,10016]{2,1,0:T(8,128)(2,1)S(1)}, u32[]{:S(2)}, u32[]{:S(2)}) collective-permute-start(bf16[2,8,10016]{2,1,0:T(8,128)(2,1)S(1)} %get-tuple-element.31), channel_id=1, source_target_pairs={{0,16},{4,20},{8,24},{12,28},{16,0},{20,4},{24,8},{28,12},{1,17},{... | collective-permute-start | bytes 961544 | tf_op jit(solution)/shard_map/ppermute | solution.py:431
  11.2 1.1 %collective-permute-start.8 = (bf16[2,8,10016]{2,1,0:T(8,128)(2,1)S(1)}, bf16[2,8,10016]{2,1,0:T(8,128)(2,1)S(1)}, u32[]{:S(2)}, u32[]{:S(2)}) collective-permute-start(bf16[2,8,10016]{2,1,0:T(8,128)(2,1)S(1)} %get-tuple-element.26.after_ref), channel_id=1, source_target_pairs={{0,24},{4,28},{8,16},{12,20},{16,8},{20,12},{24,0},{28,4},{1,25},{... | collective-permute-start | bytes 961544 | tf_op jit(solution)/shard_map/ppermute | solution.py:431
  12.3 1.2 %pack_all.1.refs_3_.home_ref = bf16[2,8,20000]{2,1,0:T(8,128)(2,1)S(1)} custom-call(s32[1]{0:T(128)} %bitcast.me_ref.other_ref.after_ref, s32[1]{0:T(128)} %bitcast.1.slab_ref, bf16[8,160000]{1,0:T(8,128)(2,1)} %bitcast.13, bf16[8,160000]{1,0:T(8,128)(2,1)S(1)} %collective-permute-done.other_ref, bf16[2,8,10016]{2,1,0:T(8,128)(2,1)S(1)} %get-tuple-element.26.after_ref), custom_call_target="tpu_custom_call" | custom-call | bytes 1280000 | tf_op jit(solution)/shard_map/pack_all/pallas_call | solution.py:84
  14.4 1.5 %collective-permute-done.4.refs_3_ = bf16[3,8,4992]{2,1,0:T(8,128)(2,1)S(1)} collective-permute-done((bf16[3,8,4992]{2,1,0:T(8,128)(2,1)S(1)}, bf16[3,8,4992]{2,1,0:T(8,128)(2,1)S(1)}, u32[]{:S(2)}, u32[]{:S(2)}) %collective-permute-start.4) | collective-permute-done | bytes 239648 | tf_op jit(solution)/shard_map/ppermute | solution.py:431
  16.0 1.6 %collective-permute-start.5 = (bf16[3,2,8,4992]{3,2,1,0:T(8,128)(2,1)S(1)}, bf16[3,2,8,4992]{3,2,1,0:T(8,128)(2,1)S(1)}, u32[]{:S(2)}, u32[]{:S(2)}) collective-permute-start(bf16[3,2,8,4992]{3,2,1,0:T(8,128)(2,1)S(1)} %join.1.refs_0_), channel_id=1, source_target_pairs={{0,1},{1,0},{2,3},{3,2},{4,5},{5,4},{6,7},{7,6},{8,9},{9,8},{10,11... | collective-permute-start | bytes 1437704 | tf_op jit(solution)/shard_map/ppermute | solution.py:431
  17.6 6.2 %mask_integrals.1 = (bf16[50,400,256]{2,1,0:T(8,128)(2,1)S(1)}, bf16[256,256]{1,0:T(8,128)(2,1)S(1)}, bf16[256,256]{1,0:T(8,128)(2,1)S(1)}, f32[8,256]{1,0:T(8,128)S(1)}) custom-call(s32[1]{0:T(128)} %bitcast.me_ref.other_ref.after_ref, s32[1]{0:T(128)} %bitcast.1.slab_ref, s32[400]{0:T(512)} %irrep_ref.1, f32[8]{0:T(128)} %occ_ref.1, f32[32]{0:T(128)} %virt_ref.1, ...), custom_call_target="tpu_custom_call" | custom-call | tf_op jit(solution)/shard_map/mask_integrals/pallas_call | solution.py:177
  23.8 0.6 %contract.3.refs_3_ = f32[64,256]{1,0:T(8,128)S(1)} custom-call(s32[1]{0:T(128)} %bitcast.1.slab_ref, s32[1]{0:T(128)} %bitcast.me_ref.other_ref.after_ref, bf16[2,8,20000]{2,1,0:T(8,128)(2,1)S(1)} %pack_all.1.refs_3_.home_ref, bf16[20000,256]{1,0:T(8,128)(2,1)S(1)} %bitcast.7, bf16[3,2,8,4992]{3,2,1,0:T(8,128)(2,1)S(1)} %join.1.refs_0_), custom_call_target="tpu_custom_call" | custom-call | flops 163577856 | bytes 3194880 | tf_op jit(solution)/shard_map/contract/pallas_call | solution.py:360
  24.4 3.5 %collective-permute-done.7.refs_1_ = bf16[2,8,10016]{2,1,0:T(8,128)(2,1)S(1)} collective-permute-done((bf16[2,8,10016]{2,1,0:T(8,128)(2,1)S(1)}, bf16[2,8,10016]{2,1,0:T(8,128)(2,1)S(1)}, u32[]{:S(2)}, u32[]{:S(2)}) %collective-permute-start.7) | collective-permute-done | bytes 320544 | tf_op jit(solution)/shard_map/ppermute | solution.py:431
  28.0 1.0 %contract.4.refs_1_ = f32[64,256]{1,0:T(8,128)S(1)} custom-call(s32[1]{0:T(128)} %bitcast.1.slab_ref, s32[1]{0:T(128)} %bitcast.me_ref.other_ref.after_ref, bf16[2,8,20000]{2,1,0:T(8,128)(2,1)S(1)} %pack_all.1.refs_3_.home_ref, bf16[20000,256]{1,0:T(8,128)(2,1)S(1)} %bitcast.8, bf16[2,8,10016]{2,1,0:T(8,128)(2,1)S(1)} %get-tuple-element.33.refs_0_, ...), custom_call_target="tpu_custom_call" | custom-call | flops 328204288 | bytes 6410240 | tf_op jit(solution)/shard_map/contract/pallas_call | solution.py:360
  29.0 0.6 %contract.5 = (f32[4,8,256]{2,1,0:T(8,128)S(1)}, f32[4,8,256]{2,1,0:T(8,128)S(1)}, f32[64,256]{1,0:T(8,128)S(1)}) custom-call(s32[1]{0:T(128)} %bitcast.1.slab_ref, s32[1]{0:T(128)} %bitcast.me_ref.other_ref.after_ref, bf16[2,8,20000]{2,1,0:T(8,128)(2,1)S(1)} %pack_all.1.refs_3_.home_ref, bf16[20000,256]{1,0:T(8,128)(2,1)S(1)} %bitcast.9, ...), custom_call_target="tpu_custom_call" | custom-call | flops 163577856 | bytes 3194880 | tf_op jit(solution)/shard_map/contract/pallas_call | solution.py:360
  29.8 1.0 %mirror_blocks.1.refs_0_ = f32[32,4,128]{2,1,0:T(4,128)} custom-call(s32[1]{0:T(128)} %bitcast.me_ref.other_ref.after_ref, f32[64,256]{1,0:T(8,128)S(1)} %get-tuple-element.36.total_ref, bf16[256,256]{1,0:T(8,128)(2,1)S(1)} %get-tuple-element.37.select_ref), custom_call_target="tpu_custom_call" | custom-call | flops 25165824 | bytes 131072 | tf_op jit(solution)/shard_map/mirror_blocks/pallas_call | solution.py:336
  30.9 5.4 %all-to-all-start = ((f32[32,4,128]{2,1,0:T(4,128)}), f32[32,4,128]{2,1,0:T(4,128)S(1)}, u32[]{:S(2)}, u32[]{:S(2)}) async-start(f32[32,4,128]{2,1,0:T(4,128)} %tie.3), calls=%async_computation | async-start | bytes 131072 | tf_op jit(solution)/shard_map/all_to_all | solution.py:470
  36.3 2.7 %collective-permute-start.10 = (f32[8,256]{1,0:T(8,128)S(1)}, f32[8,256]{1,0:T(8,128)S(1)}, u32[]{:S(2)}, u32[]{:S(2)}) collective-permute-start(f32[8,256]{1,0:T(8,128)S(1)} %get-tuple-element.42), channel_id=1, source_target_pairs={{0,24},{4,28},{8,16},{12,20},{16,8},{20,12},{24,0},{28,4},{1,25},{... | collective-permute-start | bytes 24584 | tf_op jit(solution)/shard_map/ppermute | solution.py:431
  39.0 0.6 %collective-permute-start.11 = (f32[8,256]{1,0:T(8,128)S(1)}, f32[8,256]{1,0:T(8,128)S(1)}, u32[]{:S(2)}, u32[]{:S(2)}) collective-permute-start(f32[8,256]{1,0:T(8,128)S(1)} %get-tuple-element.43), channel_id=1, source_target_pairs={{0,16},{4,20},{8,24},{12,28},{16,0},{20,4},{24,8},{28,12},{1,17},{... | collective-permute-start | bytes 24584 | tf_op jit(solution)/shard_map/ppermute | solution.py:431
  39.8 1.1 %collective-permute-done.10.refs_1_ = f32[8,256]{1,0:T(8,128)S(1)} collective-permute-done((f32[8,256]{1,0:T(8,128)S(1)}, f32[8,256]{1,0:T(8,128)S(1)}, u32[]{:S(2)}, u32[]{:S(2)}) %collective-permute-start.10) | collective-permute-done | bytes 8224 | tf_op jit(solution)/shard_map/ppermute | solution.py:431
  40.9 1.8 %collective-permute-done.11.refs_2_ = f32[8,256]{1,0:T(8,128)S(1)} collective-permute-done((f32[8,256]{1,0:T(8,128)S(1)}, f32[8,256]{1,0:T(8,128)S(1)}, u32[]{:S(2)}, u32[]{:S(2)}) %collective-permute-start.11) | collective-permute-done | bytes 8224 | tf_op jit(solution)/shard_map/ppermute | solution.py:431
  42.7 0.5 %collective-permute-done.12.refs_3_ = f32[8,256]{1,0:T(8,128)S(1)} collective-permute-done((f32[8,256]{1,0:T(8,128)S(1)}, f32[8,256]{1,0:T(8,128)S(1)}, u32[]{:S(2)}, u32[]{:S(2)}) %collective-permute-start.12) | collective-permute-done | bytes 8224 | tf_op jit(solution)/shard_map/ppermute | solution.py:431
  43.2 0.5 %all-to-all-done.mirror_ref = f32[32,4,128]{2,1,0:T(4,128)S(1)} async-done(((f32[32,4,128]{2,1,0:T(4,128)}), f32[32,4,128]{2,1,0:T(4,128)S(1)}, u32[]{:S(2)}, u32[]{:S(2)}) %all-to-all-start) | async-done | bytes 65568 | tf_op jit(solution)/shard_map/all_to_all | solution.py:470
  43.8 1.0 %finish.1 = f32[8,8,32]{2,1,0:T(8,128)} custom-call(f32[32,4,128]{2,1,0:T(4,128)S(1)} %all-to-all-done.mirror_ref, f32[8,256]{1,0:T(8,128)S(1)} %get-tuple-element.32.refs_3_.denominator_ref, bf16[256,256]{1,0:T(8,128)(2,1)S(1)} %get-tuple-element.39.select_ref, f32[8,256]{1,0:T(8,128)S(1)} %get-tuple-element.41.refs_0_, ...), custom_call_target="tpu_custom_call" | custom-call | flops 3145728 | bytes 131072 | tf_op jit(solution)/shard_map/finish/pallas_call | solution.py:419
  (18 shorter events, 2.1 us)
Async XLA Ops:
  0.0 6.0 %collective-permute-start = (bf16[8,160000]{1,0:T(8,128)(2,1)}, bf16[8,160000]{1,0:T(8,128)(2,1)S(1)}, u32[]{:S(2)}, u32[]{:S(2)}) collective-permute-start(bf16[8,160000]{1,0:T(8,128)(2,1)} %bitcast.10), channel_id=1, source_target_pairs={{0,4},{4,0},{8,12},{12,8},{16,20},{20,16},{24,28},{28,24},{1,5},{5... | collective-permute-start | bytes 7680008 | tf_op jit(solution)/shard_map/ppermute | solution.py:431
  1.9 9.3 %collective-permute-start.1 = (bf16[2,8,4992]{2,1,0:T(8,128)(2,1)S(1)}, bf16[2,8,4992]{2,1,0:T(8,128)(2,1)S(1)}, u32[]{:S(2)}, u32[]{:S(2)}) collective-permute-start(bf16[2,8,4992]{2,1,0:T(8,128)(2,1)S(1)} %get-tuple-element.27), channel_id=1, source_target_pairs={{0,8},{4,12},{8,0},{12,4},{16,24},{20,28},{24,16},{28,20},{1,9},{5... | collective-permute-start | bytes 479240 | tf_op jit(solution)/shard_map/ppermute | solution.py:431
  4.4 9.4 %collective-permute-start.2 = (bf16[2,8,4992]{2,1,0:T(8,128)(2,1)S(1)}, bf16[2,8,4992]{2,1,0:T(8,128)(2,1)S(1)}, u32[]{:S(2)}, u32[]{:S(2)}) collective-permute-start(bf16[2,8,4992]{2,1,0:T(8,128)(2,1)S(1)} %get-tuple-element.28), channel_id=1, source_target_pairs={{0,16},{4,20},{8,24},{12,28},{16,0},{20,4},{24,8},{28,12},{1,17},{... | collective-permute-start | bytes 479240 | tf_op jit(solution)/shard_map/ppermute | solution.py:431
  5.9 8.4 %collective-permute-start.3 = (bf16[2,8,4992]{2,1,0:T(8,128)(2,1)S(1)}, bf16[2,8,4992]{2,1,0:T(8,128)(2,1)S(1)}, u32[]{:S(2)}, u32[]{:S(2)}) collective-permute-start(bf16[2,8,4992]{2,1,0:T(8,128)(2,1)S(1)} %get-tuple-element.25.after_ref), channel_id=1, source_target_pairs={{0,24},{4,28},{8,16},{12,20},{16,8},{20,12},{24,0},{28,4},{1,25},{... | collective-permute-start | bytes 479240 | tf_op jit(solution)/shard_map/ppermute | solution.py:431
  7.8 16.6 %collective-permute-start.6 = (bf16[2,8,10016]{2,1,0:T(8,128)(2,1)S(1)}, bf16[2,8,10016]{2,1,0:T(8,128)(2,1)S(1)}, u32[]{:S(2)}, u32[]{:S(2)}) collective-permute-start(bf16[2,8,10016]{2,1,0:T(8,128)(2,1)S(1)} %get-tuple-element.30), channel_id=1, source_target_pairs={{0,8},{4,12},{8,0},{12,4},{16,24},{20,28},{24,16},{28,20},{1,9},{5... | collective-permute-start | bytes 961544 | tf_op jit(solution)/shard_map/ppermute | solution.py:431
  9.8 18.1 %collective-permute-start.7 = (bf16[2,8,10016]{2,1,0:T(8,128)(2,1)S(1)}, bf16[2,8,10016]{2,1,0:T(8,128)(2,1)S(1)}, u32[]{:S(2)}, u32[]{:S(2)}) collective-permute-start(bf16[2,8,10016]{2,1,0:T(8,128)(2,1)S(1)} %get-tuple-element.31), channel_id=1, source_target_pairs={{0,16},{4,20},{8,24},{12,28},{16,0},{20,4},{24,8},{28,12},{1,17},{... | collective-permute-start | bytes 961544 | tf_op jit(solution)/shard_map/ppermute | solution.py:431
  11.2 16.8 %collective-permute-start.8 = (bf16[2,8,10016]{2,1,0:T(8,128)(2,1)S(1)}, bf16[2,8,10016]{2,1,0:T(8,128)(2,1)S(1)}, u32[]{:S(2)}, u32[]{:S(2)}) collective-permute-start(bf16[2,8,10016]{2,1,0:T(8,128)(2,1)S(1)} %get-tuple-element.26.after_ref), channel_id=1, source_target_pairs={{0,24},{4,28},{8,16},{12,20},{16,8},{20,12},{24,0},{28,4},{1,25},{... | collective-permute-start | bytes 961544 | tf_op jit(solution)/shard_map/ppermute | solution.py:431
  14.4 1.6 %collective-permute-start.4 = (bf16[3,8,4992]{2,1,0:T(8,128)(2,1)S(1)}, bf16[3,8,4992]{2,1,0:T(8,128)(2,1)S(1)}, u32[]{:S(2)}, u32[]{:S(2)}) collective-permute-start(bf16[3,8,4992]{2,1,0:T(8,128)(2,1)S(1)} %take_other.1), channel_id=1, source_target_pairs={{0,4},{4,0},{8,12},{12,8},{16,20},{20,16},{24,28},{28,24},{1,5},{5... | collective-permute-start | bytes 718856 | tf_op jit(solution)/shard_map/ppermute | solution.py:431
  16.0 13.1 %collective-permute-start.5 = (bf16[3,2,8,4992]{3,2,1,0:T(8,128)(2,1)S(1)}, bf16[3,2,8,4992]{3,2,1,0:T(8,128)(2,1)S(1)}, u32[]{:S(2)}, u32[]{:S(2)}) collective-permute-start(bf16[3,2,8,4992]{3,2,1,0:T(8,128)(2,1)S(1)} %join.1.refs_0_), channel_id=1, source_target_pairs={{0,1},{1,0},{2,3},{3,2},{4,5},{5,4},{6,7},{7,6},{8,9},{9,8},{10,11... | collective-permute-start | bytes 1437704 | tf_op jit(solution)/shard_map/ppermute | solution.py:431
  29.6 1.3 %collective-permute-start.9 = (f32[4,8,256]{2,1,0:T(8,128)S(1)}, f32[4,8,256]{2,1,0:T(8,128)S(1)}, u32[]{:S(2)}, u32[]{:S(2)}) collective-permute-start(f32[4,8,256]{2,1,0:T(8,128)S(1)} %get-tuple-element.38), channel_id=1, source_target_pairs={{0,4},{4,0},{8,12},{12,8},{16,20},{20,16},{24,28},{28,24},{1,5},{5... | collective-permute-start | bytes 98312 | tf_op jit(solution)/shard_map/ppermute | solution.py:431
  30.9 12.9 %all-to-all-start = ((f32[32,4,128]{2,1,0:T(4,128)}), f32[32,4,128]{2,1,0:T(4,128)S(1)}, u32[]{:S(2)}, u32[]{:S(2)}) async-start(f32[32,4,128]{2,1,0:T(4,128)} %tie.3), calls=%async_computation | async-start | bytes 131072 | tf_op jit(solution)/shard_map/all_to_all | solution.py:470
  36.3 4.6 %collective-permute-start.10 = (f32[8,256]{1,0:T(8,128)S(1)}, f32[8,256]{1,0:T(8,128)S(1)}, u32[]{:S(2)}, u32[]{:S(2)}) collective-permute-start(f32[8,256]{1,0:T(8,128)S(1)} %get-tuple-element.42), channel_id=1, source_target_pairs={{0,24},{4,28},{8,16},{12,20},{16,8},{20,12},{24,0},{28,4},{1,25},{... | collective-permute-start | bytes 24584 | tf_op jit(solution)/shard_map/ppermute | solution.py:431
  39.0 3.7 %collective-permute-start.11 = (f32[8,256]{1,0:T(8,128)S(1)}, f32[8,256]{1,0:T(8,128)S(1)}, u32[]{:S(2)}, u32[]{:S(2)}) collective-permute-start(f32[8,256]{1,0:T(8,128)S(1)} %get-tuple-element.43), channel_id=1, source_target_pairs={{0,16},{4,20},{8,24},{12,28},{16,0},{20,4},{24,8},{28,12},{1,17},{... | collective-permute-start | bytes 24584 | tf_op jit(solution)/shard_map/ppermute | solution.py:431
  39.6 3.7 %collective-permute-start.12 = (f32[8,256]{1,0:T(8,128)S(1)}, f32[8,256]{1,0:T(8,128)S(1)}, u32[]{:S(2)}, u32[]{:S(2)}) collective-permute-start(f32[8,256]{1,0:T(8,128)S(1)} %get-tuple-element.44), channel_id=1, source_target_pairs={{0,8},{4,12},{8,0},{12,4},{16,24},{20,28},{24,16},{28,20},{1,9},{5... | collective-permute-start | bytes 24584 | tf_op jit(solution)/shard_map/ppermute | solution.py:431
where the time goes:
time: 45.1 us; the launch traced here: 44.8 us
  starting transfers between devices  19.8 us (44%)
  Pallas kernels  15 us (33%)
  waiting for transfers between devices  9.94 us (22%)
    ppermute x13, starting transfers between devices, swap(): lax.ppermute(values, axis, [(p, p ^ bits) for p in range(lax.axis_size(ax...  14.4 us
    ppermute x13, waiting for transfers between devices, swap(): lax.ppermute(values, axis, [(p, p ^ bits) for p in range(lax.axis_size(ax...  9.4 us
    pallas_call x1, Pallas kernels, mask(): pl.pallas_call(functools.partial(mask_kernel, per_step, parts), grid=(chu...  6.23 us
    all_to_all x1, starting transfers between devices, local(): lax.all_to_all(mirror, ('pair', 'slab'), split_axis=0, concat_axis=0, til...  5.37 us
    pallas_call x3, Pallas kernels, pack(): pl.pallas_call(functools.partial(pack_kernel, rows_local, shared, which),...  4.42 us
    pallas_call x3, Pallas kernels, contract(): pl.pallas_call(functools.partial(contract_kernel, which, shared), out_sha...  2.21 us
    pallas_call x1, Pallas kernels, finish(): pl.pallas_call(finish_kernel, out_shape=jax.ShapeDtypeStruct((rows, first...  1.04 us
    pallas_call x1, Pallas kernels, mirror_blocks(): pl.pallas_call(mirror_kernel, out_shape=jax.ShapeDtypeStruct((count * sla...  1.01 us
  transfers between devices with their start and end apart: 14, of which 9 were waited for; matrix products, arithmetic and copies ran while one was open for 0% of the time, Pallas kernels for 30%

commit v1 on v0

--- a/solution.py
+++ b/solution.py
@@ -58,16 +58,18 @@
                 load(dest, source).wait()
                 block = held[slots(dest), source, :, shift : shift + size]
                 if which == "own":
-                    packed[dest ^ me] = block
+                    for k, out in enumerate(outs):
+
+                        @pl.when((dest ^ me) // 2 == k + 1)
+                        def _():
+                            out[(dest ^ me) & 1] = block
+
                 elif which == "rest":
                     packed[(dest ^ me) // 2, source] = block
                 else:
                     outs[0][source] = block
 
-    if which == "own":
-        for k, out in enumerate(outs):
-            out[...] = packed[2 * k + 2 : 2 * k + 4]
-    elif which == "rest":
+    if which == "rest":
         for k, out in enumerate(outs):
             out[...] = packed[k + 1]
 
@@ -79,7 +81,7 @@
     slots = {"own": pair_count, "rest": pair_count // 2, "all": 1}[which]
     sources = 1 if which == "own" else 2
     held = (slots, sources, rows, -(-size // 128) * 128 + 128)
-    packed = {"own": (pair_count, rows, size), "rest": (pair_count // 2, 2, rows, size), "all": (1, rows, size)}[which]
+    packed = {"own": (1, rows, size), "rest": (pair_count // 2, 2, rows, size), "all": (1, rows, size)}[which]
     outs = 1 if which == "all" else pair_count // 2 - 1
     return pl.pallas_call(
         functools.partial(pack_kernel, rows_local, shared, which),

time: 45.1 us -> 45.1 us (level)
  no operation moved by 1% of the time
where the time goes in v1:
time: 45.1 us; the launch traced here: 44.8 us
  starting transfers between devices  19.8 us (44%)
  Pallas kernels  15 us (33%)
  waiting for transfers between devices  9.94 us (22%)
    ppermute x13, starting transfers between devices, swap(): lax.ppermute(values, axis, [(p, p ^ bits) for p in range(lax.axis_size(ax...  14.4 us
    ppermute x13, waiting for transfers between devices, swap(): lax.ppermute(values, axis, [(p, p ^ bits) for p in range(lax.axis_size(ax...  9.4 us
    pallas_call x1, Pallas kernels, mask(): pl.pallas_call(functools.partial(mask_kernel, per_step, parts), grid=(chu...  6.23 us
    all_to_all x1, starting transfers between devices, local(): lax.all_to_all(mirror, ('pair', 'slab'), split_axis=0, concat_axis=0, til...  5.37 us
    pallas_call x3, Pallas kernels, pack(): pl.pallas_call(functools.partial(pack_kernel, rows_local, shared, which),...  4.47 us
    pallas_call x3, Pallas kernels, contract(): pl.pallas_call(functools.partial(contract_kernel, which, shared), out_sha...  2.22 us
    pallas_call x1, Pallas kernels, finish(): pl.pallas_call(finish_kernel, out_shape=jax.ShapeDtypeStruct((rows, first...  1.04 us
    pallas_call x1, Pallas kernels, mirror_blocks(): pl.pallas_call(mirror_kernel, out_shape=jax.ShapeDtypeStruct((count * sla...  1.01 us
  transfers between devices with their start and end apart: 14, of which 9 were waited for; matrix products, arithmetic and copies ran while one was open for 0% of the time, Pallas kernels for 30%

profile of v1, /device:TPU:0, one launch (start us, length us, event | category | flops | bytes accessed | tf_op | source)
XLA Modules:
  0.0 44.8 jit_solution(14127916200694804381)
XLA Ops:
  0.5 1.5 %pack_own.1 = (bf16[2,8,4992]{2,1,0:T(8,128)(2,1)S(1)}, bf16[2,8,4992]{2,1,0:T(8,128)(2,1)S(1)}, bf16[2,8,4992]{2,1,0:T(8,128)(2,1)S(1)}) custom-call(s32[1]{0:T(128)} %bitcast.me_ref.other_ref.after_ref, s32[1]{0:T(128)} %bitcast.1.slab_ref, bf16[8,160000]{1,0:T(8,128)(2,1)} %bitcast.11, s32[1]{0:T(128)} %bitcast.me_ref.other_ref.after_ref, ...), custom_call_target="tpu_custom_call" | custom-call | bytes 1277952 | tf_op jit(solution)/shard_map/pack_own/pallas_call | solution.py:86
  2.0 2.5 %collective-permute-start.1 = (bf16[2,8,4992]{2,1,0:T(8,128)(2,1)S(1)}, bf16[2,8,4992]{2,1,0:T(8,128)(2,1)S(1)}, u32[]{:S(2)}, u32[]{:S(2)}) collective-permute-start(bf16[2,8,4992]{2,1,0:T(8,128)(2,1)S(1)} %get-tuple-element.27), channel_id=1, source_target_pairs={{0,8},{4,12},{8,0},{12,4},{16,24},{20,28},{24,16},{28,20},{1,9},{5... | collective-permute-start | bytes 479240 | tf_op jit(solution)/shard_map/ppermute | solution.py:433
  4.4 1.5 %collective-permute-start.2 = (bf16[2,8,4992]{2,1,0:T(8,128)(2,1)S(1)}, bf16[2,8,4992]{2,1,0:T(8,128)(2,1)S(1)}, u32[]{:S(2)}, u32[]{:S(2)}) collective-permute-start(bf16[2,8,4992]{2,1,0:T(8,128)(2,1)S(1)} %get-tuple-element.28), channel_id=1, source_target_pairs={{0,16},{4,20},{8,24},{12,28},{16,0},{20,4},{24,8},{28,12},{1,17},{... | collective-permute-start | bytes 479240 | tf_op jit(solution)/shard_map/ppermute | solution.py:433
  6.0 1.8 %pack_rest.1 = (bf16[2,8,10016]{2,1,0:T(8,128)(2,1)S(1)}, bf16[2,8,10016]{2,1,0:T(8,128)(2,1)S(1)}, bf16[2,8,10016]{2,1,0:T(8,128)(2,1)S(1)}) custom-call(s32[1]{0:T(128)} %bitcast.me_ref.other_ref.after_ref, s32[1]{0:T(128)} %bitcast.1.slab_ref, bf16[8,160000]{1,0:T(8,128)(2,1)} %bitcast.12, bf16[8,160000]{1,0:T(8,128)(2,1)S(1)} %collective-permute-done.other_ref, ...), custom_call_target="tpu_custom_call" | custom-call | bytes 2564096 | tf_op jit(solution)/shard_map/pack_rest/pallas_call | solution.py:86
  7.8 2.0 %collective-permute-start.6 = (bf16[2,8,10016]{2,1,0:T(8,128)(2,1)S(1)}, bf16[2,8,10016]{2,1,0:T(8,128)(2,1)S(1)}, u32[]{:S(2)}, u32[]{:S(2)}) collective-permute-start(bf16[2,8,10016]{2,1,0:T(8,128)(2,1)S(1)} %get-tuple-element.30), channel_id=1, source_target_pairs={{0,8},{4,12},{8,0},{12,4},{16,24},{20,28},{24,16},{28,20},{1,9},{5... | collective-permute-start | bytes 961544 | tf_op jit(solution)/shard_map/ppermute | solution.py:433
  9.8 1.3 %collective-permute-start.7 = (bf16[2,8,10016]{2,1,0:T(8,128)(2,1)S(1)}, bf16[2,8,10016]{2,1,0:T(8,128)(2,1)S(1)}, u32[]{:S(2)}, u32[]{:S(2)}) collective-permute-start(bf16[2,8,10016]{2,1,0:T(8,128)(2,1)S(1)} %get-tuple-element.31), channel_id=1, source_target_pairs={{0,16},{4,20},{8,24},{12,28},{16,0},{20,4},{24,8},{28,12},{1,17},{... | collective-permute-start | bytes 961544 | tf_op jit(solution)/shard_map/ppermute | solution.py:433
  11.2 1.1 %collective-permute-start.8 = (bf16[2,8,10016]{2,1,0:T(8,128)(2,1)S(1)}, bf16[2,8,10016]{2,1,0:T(8,128)(2,1)S(1)}, u32[]{:S(2)}, u32[]{:S(2)}) collective-permute-start(bf16[2,8,10016]{2,1,0:T(8,128)(2,1)S(1)} %get-tuple-element.26.after_ref), channel_id=1, source_target_pairs={{0,24},{4,28},{8,16},{12,20},{16,8},{20,12},{24,0},{28,4},{1,25},{... | collective-permute-start | bytes 961544 | tf_op jit(solution)/shard_map/ppermute | solution.py:433
  12.3 1.2 %pack_all.1.refs_3_.home_ref = bf16[2,8,20000]{2,1,0:T(8,128)(2,1)S(1)} custom-call(s32[1]{0:T(128)} %bitcast.me_ref.other_ref.after_ref, s32[1]{0:T(128)} %bitcast.1.slab_ref, bf16[8,160000]{1,0:T(8,128)(2,1)} %bitcast.13, bf16[8,160000]{1,0:T(8,128)(2,1)S(1)} %collective-permute-done.other_ref, bf16[2,8,10016]{2,1,0:T(8,128)(2,1)S(1)} %get-tuple-element.26.after_ref), custom_call_target="tpu_custom_call" | custom-call | bytes 1280000 | tf_op jit(solution)/shard_map/pack_all/pallas_call | solution.py:86
  14.5 1.5 %collective-permute-done.4.refs_3_ = bf16[3,8,4992]{2,1,0:T(8,128)(2,1)S(1)} collective-permute-done((bf16[3,8,4992]{2,1,0:T(8,128)(2,1)S(1)}, bf16[3,8,4992]{2,1,0:T(8,128)(2,1)S(1)}, u32[]{:S(2)}, u32[]{:S(2)}) %collective-permute-start.4) | collective-permute-done | bytes 239648 | tf_op jit(solution)/shard_map/ppermute | solution.py:433
  16.0 1.6 %collective-permute-start.5 = (bf16[3,2,8,4992]{3,2,1,0:T(8,128)(2,1)S(1)}, bf16[3,2,8,4992]{3,2,1,0:T(8,128)(2,1)S(1)}, u32[]{:S(2)}, u32[]{:S(2)}) collective-permute-start(bf16[3,2,8,4992]{3,2,1,0:T(8,128)(2,1)S(1)} %join.1.refs_0_), channel_id=1, source_target_pairs={{0,1},{1,0},{2,3},{3,2},{4,5},{5,4},{6,7},{7,6},{8,9},{9,8},{10,11... | collective-permute-start | bytes 1437704 | tf_op jit(solution)/shard_map/ppermute | solution.py:433
  17.6 6.2 %mask_integrals.1 = (bf16[50,400,256]{2,1,0:T(8,128)(2,1)S(1)}, bf16[256,256]{1,0:T(8,128)(2,1)S(1)}, bf16[256,256]{1,0:T(8,128)(2,1)S(1)}, f32[8,256]{1,0:T(8,128)S(1)}) custom-call(s32[1]{0:T(128)} %bitcast.me_ref.other_ref.after_ref, s32[1]{0:T(128)} %bitcast.1.slab_ref, s32[400]{0:T(512)} %irrep_ref.1, f32[8]{0:T(128)} %occ_ref.1, f32[32]{0:T(128)} %virt_ref.1, ...), custom_call_target="tpu_custom_call" | custom-call | tf_op jit(solution)/shard_map/mask_integrals/pallas_call | solution.py:179
  23.9 0.6 %contract.3.refs_3_ = f32[64,256]{1,0:T(8,128)S(1)} custom-call(s32[1]{0:T(128)} %bitcast.1.slab_ref, s32[1]{0:T(128)} %bitcast.me_ref.other_ref.after_ref, bf16[2,8,20000]{2,1,0:T(8,128)(2,1)S(1)} %pack_all.1.refs_3_.home_ref, bf16[20000,256]{1,0:T(8,128)(2,1)S(1)} %bitcast.7, bf16[3,2,8,4992]{3,2,1,0:T(8,128)(2,1)S(1)} %join.1.refs_0_), custom_call_target="tpu_custom_call" | custom-call | flops 163577856 | bytes 3194880 | tf_op jit(solution)/shard_map/contract/pallas_call | solution.py:362
  24.5 3.5 %collective-permute-done.7.refs_1_ = bf16[2,8,10016]{2,1,0:T(8,128)(2,1)S(1)} collective-permute-done((bf16[2,8,10016]{2,1,0:T(8,128)(2,1)S(1)}, bf16[2,8,10016]{2,1,0:T(8,128)(2,1)S(1)}, u32[]{:S(2)}, u32[]{:S(2)}) %collective-permute-start.7) | collective-permute-done | bytes 320544 | tf_op jit(solution)/shard_map/ppermute | solution.py:433
  28.0 1.0 %contract.4.refs_1_ = f32[64,256]{1,0:T(8,128)S(1)} custom-call(s32[1]{0:T(128)} %bitcast.1.slab_ref, s32[1]{0:T(128)} %bitcast.me_ref.other_ref.after_ref, bf16[2,8,20000]{2,1,0:T(8,128)(2,1)S(1)} %pack_all.1.refs_3_.home_ref, bf16[20000,256]{1,0:T(8,128)(2,1)S(1)} %bitcast.8, bf16[2,8,10016]{2,1,0:T(8,128)(2,1)S(1)} %get-tuple-element.33.refs_0_, ...), custom_call_target="tpu_custom_call" | custom-call | flops 328204288 | bytes 6410240 | tf_op jit(solution)/shard_map/contract/pallas_call | solution.py:362
  29.0 0.6 %contract.5 = (f32[4,8,256]{2,1,0:T(8,128)S(1)}, f32[4,8,256]{2,1,0:T(8,128)S(1)}, f32[64,256]{1,0:T(8,128)S(1)}) custom-call(s32[1]{0:T(128)} %bitcast.1.slab_ref, s32[1]{0:T(128)} %bitcast.me_ref.other_ref.after_ref, bf16[2,8,20000]{2,1,0:T(8,128)(2,1)S(1)} %pack_all.1.refs_3_.home_ref, bf16[20000,256]{1,0:T(8,128)(2,1)S(1)} %bitcast.9, ...), custom_call_target="tpu_custom_call" | custom-call | flops 163577856 | bytes 3194880 | tf_op jit(solution)/shard_map/contract/pallas_call | solution.py:362
  29.8 1.0 %mirror_blocks.1.refs_0_ = f32[32,4,128]{2,1,0:T(4,128)} custom-call(s32[1]{0:T(128)} %bitcast.me_ref.other_ref.after_ref, f32[64,256]{1,0:T(8,128)S(1)} %get-tuple-element.36.total_ref, bf16[256,256]{1,0:T(8,128)(2,1)S(1)} %get-tuple-element.37.select_ref), custom_call_target="tpu_custom_call" | custom-call | flops 25165824 | bytes 131072 | tf_op jit(solution)/shard_map/mirror_blocks/pallas_call | solution.py:338
  30.9 5.4 %all-to-all-start = ((f32[32,4,128]{2,1,0:T(4,128)}), f32[32,4,128]{2,1,0:T(4,128)S(1)}, u32[]{:S(2)}, u32[]{:S(2)}) async-start(f32[32,4,128]{2,1,0:T(4,128)} %tie.3), calls=%async_computation | async-start | bytes 131072 | tf_op jit(solution)/shard_map/all_to_all | solution.py:472
  36.3 2.7 %collective-permute-start.10 = (f32[8,256]{1,0:T(8,128)S(1)}, f32[8,256]{1,0:T(8,128)S(1)}, u32[]{:S(2)}, u32[]{:S(2)}) collective-permute-start(f32[8,256]{1,0:T(8,128)S(1)} %get-tuple-element.42), channel_id=1, source_target_pairs={{0,24},{4,28},{8,16},{12,20},{16,8},{20,12},{24,0},{28,4},{1,25},{... | collective-permute-start | bytes 24584 | tf_op jit(solution)/shard_map/ppermute | solution.py:433
  39.1 0.6 %collective-permute-start.11 = (f32[8,256]{1,0:T(8,128)S(1)}, f32[8,256]{1,0:T(8,128)S(1)}, u32[]{:S(2)}, u32[]{:S(2)}) collective-permute-start(f32[8,256]{1,0:T(8,128)S(1)} %get-tuple-element.43), channel_id=1, source_target_pairs={{0,16},{4,20},{8,24},{12,28},{16,0},{20,4},{24,8},{28,12},{1,17},{... | collective-permute-start | bytes 24584 | tf_op jit(solution)/shard_map/ppermute | solution.py:433
  39.9 1.1 %collective-permute-done.10.refs_1_ = f32[8,256]{1,0:T(8,128)S(1)} collective-permute-done((f32[8,256]{1,0:T(8,128)S(1)}, f32[8,256]{1,0:T(8,128)S(1)}, u32[]{:S(2)}, u32[]{:S(2)}) %collective-permute-start.10) | collective-permute-done | bytes 8224 | tf_op jit(solution)/shard_map/ppermute | solution.py:433
  40.9 1.8 %collective-permute-done.11.refs_2_ = f32[8,256]{1,0:T(8,128)S(1)} collective-permute-done((f32[8,256]{1,0:T(8,128)S(1)}, f32[8,256]{1,0:T(8,128)S(1)}, u32[]{:S(2)}, u32[]{:S(2)}) %collective-permute-start.11) | collective-permute-done | bytes 8224 | tf_op jit(solution)/shard_map/ppermute | solution.py:433
  42.7 0.5 %collective-permute-done.12.refs_3_ = f32[8,256]{1,0:T(8,128)S(1)} collective-permute-done((f32[8,256]{1,0:T(8,128)S(1)}, f32[8,256]{1,0:T(8,128)S(1)}, u32[]{:S(2)}, u32[]{:S(2)}) %collective-permute-start.12) | collective-permute-done | bytes 8224 | tf_op jit(solution)/shard_map/ppermute | solution.py:433
  43.3 0.5 %all-to-all-done.mirror_ref = f32[32,4,128]{2,1,0:T(4,128)S(1)} async-done(((f32[32,4,128]{2,1,0:T(4,128)}), f32[32,4,128]{2,1,0:T(4,128)S(1)}, u32[]{:S(2)}, u32[]{:S(2)}) %all-to-all-start) | async-done | bytes 65568 | tf_op jit(solution)/shard_map/all_to_all | solution.py:472
  43.8 1.0 %finish.1 = f32[8,8,32]{2,1,0:T(8,128)} custom-call(f32[32,4,128]{2,1,0:T(4,128)S(1)} %all-to-all-done.mirror_ref, f32[8,256]{1,0:T(8,128)S(1)} %get-tuple-element.32.refs_3_.denominator_ref, bf16[256,256]{1,0:T(8,128)(2,1)S(1)} %get-tuple-element.39.select_ref, f32[8,256]{1,0:T(8,128)S(1)} %get-tuple-element.41.refs_0_, ...), custom_call_target="tpu_custom_call" | custom-call | flops 3145728 | bytes 131072 | tf_op jit(solution)/shard_map/finish/pallas_call | solution.py:421
  (18 shorter events, 2.1 us)
Async XLA Ops:
  0.0 6.0 %collective-permute-start = (bf16[8,160000]{1,0:T(8,128)(2,1)}, bf16[8,160000]{1,0:T(8,128)(2,1)S(1)}, u32[]{:S(2)}, u32[]{:S(2)}) collective-permute-start(bf16[8,160000]{1,0:T(8,128)(2,1)} %bitcast.10), channel_id=1, source_target_pairs={{0,4},{4,0},{8,12},{12,8},{16,20},{20,16},{24,28},{28,24},{1,5},{5... | collective-permute-start | bytes 7680008 | tf_op jit(solution)/shard_map/ppermute | solution.py:433
  2.0 9.2 %collective-permute-start.1 = (bf16[2,8,4992]{2,1,0:T(8,128)(2,1)S(1)}, bf16[2,8,4992]{2,1,0:T(8,128)(2,1)S(1)}, u32[]{:S(2)}, u32[]{:S(2)}) collective-permute-start(bf16[2,8,4992]{2,1,0:T(8,128)(2,1)S(1)} %get-tuple-element.27), channel_id=1, source_target_pairs={{0,8},{4,12},{8,0},{12,4},{16,24},{20,28},{24,16},{28,20},{1,9},{5... | collective-permute-start | bytes 479240 | tf_op jit(solution)/shard_map/ppermute | solution.py:433
  4.4 9.5 %collective-permute-start.2 = (bf16[2,8,4992]{2,1,0:T(8,128)(2,1)S(1)}, bf16[2,8,4992]{2,1,0:T(8,128)(2,1)S(1)}, u32[]{:S(2)}, u32[]{:S(2)}) collective-permute-start(bf16[2,8,4992]{2,1,0:T(8,128)(2,1)S(1)} %get-tuple-element.28), channel_id=1, source_target_pairs={{0,16},{4,20},{8,24},{12,28},{16,0},{20,4},{24,8},{28,12},{1,17},{... | collective-permute-start | bytes 479240 | tf_op jit(solution)/shard_map/ppermute | solution.py:433
  6.0 8.4 %collective-permute-start.3 = (bf16[2,8,4992]{2,1,0:T(8,128)(2,1)S(1)}, bf16[2,8,4992]{2,1,0:T(8,128)(2,1)S(1)}, u32[]{:S(2)}, u32[]{:S(2)}) collective-permute-start(bf16[2,8,4992]{2,1,0:T(8,128)(2,1)S(1)} %get-tuple-element.25.after_ref), channel_id=1, source_target_pairs={{0,24},{4,28},{8,16},{12,20},{16,8},{20,12},{24,0},{28,4},{1,25},{... | collective-permute-start | bytes 479240 | tf_op jit(solution)/shard_map/ppermute | solution.py:433
  7.8 16.6 %collective-permute-start.6 = (bf16[2,8,10016]{2,1,0:T(8,128)(2,1)S(1)}, bf16[2,8,10016]{2,1,0:T(8,128)(2,1)S(1)}, u32[]{:S(2)}, u32[]{:S(2)}) collective-permute-start(bf16[2,8,10016]{2,1,0:T(8,128)(2,1)S(1)} %get-tuple-element.30), channel_id=1, source_target_pairs={{0,8},{4,12},{8,0},{12,4},{16,24},{20,28},{24,16},{28,20},{1,9},{5... | collective-permute-start | bytes 961544 | tf_op jit(solution)/shard_map/ppermute | solution.py:433
  9.8 18.1 %collective-permute-start.7 = (bf16[2,8,10016]{2,1,0:T(8,128)(2,1)S(1)}, bf16[2,8,10016]{2,1,0:T(8,128)(2,1)S(1)}, u32[]{:S(2)}, u32[]{:S(2)}) collective-permute-start(bf16[2,8,10016]{2,1,0:T(8,128)(2,1)S(1)} %get-tuple-element.31), channel_id=1, source_target_pairs={{0,16},{4,20},{8,24},{12,28},{16,0},{20,4},{24,8},{28,12},{1,17},{... | collective-permute-start | bytes 961544 | tf_op jit(solution)/shard_map/ppermute | solution.py:433
  11.2 16.8 %collective-permute-start.8 = (bf16[2,8,10016]{2,1,0:T(8,128)(2,1)S(1)}, bf16[2,8,10016]{2,1,0:T(8,128)(2,1)S(1)}, u32[]{:S(2)}, u32[]{:S(2)}) collective-permute-start(bf16[2,8,10016]{2,1,0:T(8,128)(2,1)S(1)} %get-tuple-element.26.after_ref), channel_id=1, source_target_pairs={{0,24},{4,28},{8,16},{12,20},{16,8},{20,12},{24,0},{28,4},{1,25},{... | collective-permute-start | bytes 961544 | tf_op jit(solution)/shard_map/ppermute | solution.py:433
  14.4 1.6 %collective-permute-start.4 = (bf16[3,8,4992]{2,1,0:T(8,128)(2,1)S(1)}, bf16[3,8,4992]{2,1,0:T(8,128)(2,1)S(1)}, u32[]{:S(2)}, u32[]{:S(2)}) collective-permute-start(bf16[3,8,4992]{2,1,0:T(8,128)(2,1)S(1)} %take_other.1), channel_id=1, source_target_pairs={{0,4},{4,0},{8,12},{12,8},{16,20},{20,16},{24,28},{28,24},{1,5},{5... | collective-permute-start | bytes 718856 | tf_op jit(solution)/shard_map/ppermute | solution.py:433
  16.0 13.1 %collective-permute-start.5 = (bf16[3,2,8,4992]{3,2,1,0:T(8,128)(2,1)S(1)}, bf16[3,2,8,4992]{3,2,1,0:T(8,128)(2,1)S(1)}, u32[]{:S(2)}, u32[]{:S(2)}) collective-permute-start(bf16[3,2,8,4992]{3,2,1,0:T(8,128)(2,1)S(1)} %join.1.refs_0_), channel_id=1, source_target_pairs={{0,1},{1,0},{2,3},{3,2},{4,5},{5,4},{6,7},{7,6},{8,9},{9,8},{10,11... | collective-permute-start | bytes 1437704 | tf_op jit(solution)/shard_map/ppermute | solution.py:433
  29.6 1.3 %collective-permute-start.9 = (f32[4,8,256]{2,1,0:T(8,128)S(1)}, f32[4,8,256]{2,1,0:T(8,128)S(1)}, u32[]{:S(2)}, u32[]{:S(2)}) collective-permute-start(f32[4,8,256]{2,1,0:T(8,128)S(1)} %get-tuple-element.38), channel_id=1, source_target_pairs={{0,4},{4,0},{8,12},{12,8},{16,20},{20,16},{24,28},{28,24},{1,5},{5... | collective-permute-start | bytes 98312 | tf_op jit(solution)/shard_map/ppermute | solution.py:433
  30.9 12.9 %all-to-all-start = ((f32[32,4,128]{2,1,0:T(4,128)}), f32[32,4,128]{2,1,0:T(4,128)S(1)}, u32[]{:S(2)}, u32[]{:S(2)}) async-start(f32[32,4,128]{2,1,0:T(4,128)} %tie.3), calls=%async_computation | async-start | bytes 131072 | tf_op jit(solution)/shard_map/all_to_all | solution.py:472
  36.3 4.6 %collective-permute-start.10 = (f32[8,256]{1,0:T(8,128)S(1)}, f32[8,256]{1,0:T(8,128)S(1)}, u32[]{:S(2)}, u32[]{:S(2)}) collective-permute-start(f32[8,256]{1,0:T(8,128)S(1)} %get-tuple-element.42), channel_id=1, source_target_pairs={{0,24},{4,28},{8,16},{12,20},{16,8},{20,12},{24,0},{28,4},{1,25},{... | collective-permute-start | bytes 24584 | tf_op jit(solution)/shard_map/ppermute | solution.py:433
  39.1 3.7 %collective-permute-start.11 = (f32[8,256]{1,0:T(8,128)S(1)}, f32[8,256]{1,0:T(8,128)S(1)}, u32[]{:S(2)}, u32[]{:S(2)}) collective-permute-start(f32[8,256]{1,0:T(8,128)S(1)} %get-tuple-element.43), channel_id=1, source_target_pairs={{0,16},{4,20},{8,24},{12,28},{16,0},{20,4},{24,8},{28,12},{1,17},{... | collective-permute-start | bytes 24584 | tf_op jit(solution)/shard_map/ppermute | solution.py:433
  39.6 3.7 %collective-permute-start.12 = (f32[8,256]{1,0:T(8,128)S(1)}, f32[8,256]{1,0:T(8,128)S(1)}, u32[]{:S(2)}, u32[]{:S(2)}) collective-permute-start(f32[8,256]{1,0:T(8,128)S(1)} %get-tuple-element.44), channel_id=1, source_target_pairs={{0,8},{4,12},{8,0},{12,4},{16,24},{20,28},{24,16},{28,20},{1,9},{5... | collective-permute-start | bytes 24584 | tf_op jit(solution)/shard_map/ppermute | solution.py:433

commit v2 on v1

--- a/solution.py
+++ b/solution.py
@@ -283,26 +283,25 @@
     return terms[0] + terms[1] + terms[2]
 
 
-def contract_kernel(which, shared, slab_ref, me_ref, home_ref, ints_ref, *refs):
-    last = which == "other"
+def contract_kernel(passes, shared, slab_ref, me_ref, home_ref, ints_ref, *refs):
+    last = len(passes) > 1
     lhs = refs[-2] if last else refs[-1]
-    count, rows, size = lhs.shape
+    count, rows, _ = lhs.shape
     chips = count // 2 - 1
-    start = start_of(which, slab_ref, shared)
-    lhs[:2] = home_ref[:, :, pl.ds(start, size)]
-    for k in range(chips):
-        if which == "rest":
-            lhs[2 * k + 2 : 2 * k + 4] = refs[k][...]
-        else:
-            lhs[2 * k + 2 : 2 * k + 4] = refs[0][k]
-    refs = refs[chips if which == "rest" else 1 :]
-    step = 2560
     total = None
-    for first in range(0, size, step):
-        width = min(step, size - first)
-        block = lhs[:, :, first : first + width].reshape(count * rows, width)
-        part = jnp.dot(block, ints_ref[pl.ds(start + first, width)], preferred_element_type=jnp.float32)
-        total = part if total is None else total + part
+    for which in passes:
+        start = start_of(which, slab_ref, shared)
+        size = ints_ref.shape[0] - 2 * shared if which == "rest" else shared
+        lhs[:2, :, :size] = home_ref[:, :, pl.ds(start, size)]
+        for k in range(chips):
+            lhs[2 * k + 2 : 2 * k + 4, :, :size] = refs[k][...] if which == "rest" else refs[0][k]
+        refs = refs[chips if which == "rest" else 1 :]
+        step = 2560
+        for first in range(0, size, step):
+            width = min(step, size - first)
+            block = lhs[:, :, first : first + width].reshape(count * rows, width)
+            part = jnp.dot(block, ints_ref[pl.ds(start + first, width)], preferred_element_type=jnp.float32)
+            total = part if total is None else total + part
     if not last:
         before, out_ref = refs[:-2], refs[-2]
         out_ref[...] = total + before[0][...] if before else total
@@ -347,20 +346,21 @@
     )(me, total, select)
 
 
-def contract(amps, home, ints, me, slab, shared, which, before=None):
-    occupied, size = amps[0].shape[-2:]
+def contract(amps, home, ints, me, slab, shared, passes, before=None):
+    occupied = home.shape[1]
+    size = max(array.shape[-1] for array in amps)
     cols = ints.shape[1]
     vmem = pl.BlockSpec(memory_space=pltpu.VMEM)
     operands = [*amps] + ([] if before is None else [before])
     scratch = [pltpu.VMEM((occupied, occupied, size), home.dtype)]
-    if which == "other":
+    if len(passes) > 1:
         out_shape = [jax.ShapeDtypeStruct((occupied // 2, occupied, cols), jnp.float32)] * 2
         out_shape.append(jax.ShapeDtypeStruct((occupied * occupied, cols), jnp.float32))
         scratch.append(pltpu.VMEM((occupied, occupied, cols), jnp.float32))
     else:
         out_shape = [jax.ShapeDtypeStruct((occupied * occupied, cols), jnp.float32)]
     return pl.pallas_call(
-        functools.partial(contract_kernel, which, shared),
+        functools.partial(contract_kernel, passes, shared),
         out_shape=out_shape,
         in_specs=[pl.BlockSpec(memory_space=pltpu.SMEM)] * 2 + [vmem] * (2 + len(operands)),
         out_specs=[vmem] * len(out_shape),
@@ -463,9 +463,8 @@
     masked, by_slab, by_first, denominator = mask(integrals, me, slab, virt_irrep, occ_energy, slab_energy, own_amps)
     rest_amps = tie(rest_amps, denominator, TIE_FLOPS)
     place = (home, masked, me, slab, shared)
-    (partial,) = contract([own_amps], *place, "own")
-    (partial,) = contract(rest_amps, *place, "rest", partial)
-    even, odd, total = contract([other_amps], *place, "other", partial)
+    (partial,) = contract([own_amps], *place, ["own"])
+    even, odd, total = contract([*rest_amps, other_amps], *place, ["rest", "other"], partial)
 
     odd = swap(odd, "pair", 1)
     (mirror,) = tie([mirror_blocks(total, by_slab, me, slab_count)], odd)

time: 45.1 us -> 46 us (1.020)
  waiting for transfers between devices: 9.94 us -> 11.1 us
    ppermute x13, waiting for transfers between devices: 9.4 us -> 10.6 us  [swap(): lax.ppermute(values, axis, [(p, p ^ bits) for p in range(lax.axis_size(ax...]
    pallas_call x3 -> x2, Pallas kernels: 2.22 us -> 2.08 us  [contract(): pl.pallas_call(functools.partial(contract_kernel, passes, shared), out_sh...]
  transfers between devices with their start and end apart: 14 -> 14, of which waited for: 9 -> 10; matrix products, arithmetic and copies ran while one was open for 0% -> 0% of each run, Pallas kernels for 30% -> 27%
where the time goes in v2:
time: 46 us; the launch traced here: 45.7 us
  starting transfers between devices  19.7 us (43%)
  Pallas kernels  14.9 us (32%)
  waiting for transfers between devices  11.1 us (24%)
    ppermute x13, starting transfers between devices, swap(): lax.ppermute(values, axis, [(p, p ^ bits) for p in range(lax.axis_size(ax...  14.3 us
    ppermute x13, waiting for transfers between devices, swap(): lax.ppermute(values, axis, [(p, p ^ bits) for p in range(lax.axis_size(ax...  10.6 us
    pallas_call x1, Pallas kernels, mask(): pl.pallas_call(functools.partial(mask_kernel, per_step, parts), grid=(chu...  6.21 us
    all_to_all x1, starting transfers between devices, local(): lax.all_to_all(mirror, ('pair', 'slab'), split_axis=0, concat_axis=0, til...  5.37 us
    pallas_call x3, Pallas kernels, pack(): pl.pallas_call(functools.partial(pack_kernel, rows_local, shared, which),...  4.47 us
    pallas_call x2, Pallas kernels, contract(): pl.pallas_call(functools.partial(contract_kernel, passes, shared), out_sh...  2.08 us
    pallas_call x1, Pallas kernels, finish(): pl.pallas_call(finish_kernel, out_shape=jax.ShapeDtypeStruct((rows, first...  1.04 us
    pallas_call x1, Pallas kernels, mirror_blocks(): pl.pallas_call(mirror_kernel, out_shape=jax.ShapeDtypeStruct((count * sla...  1.01 us
  transfers between devices with their start and end apart: 14, of which 10 were waited for; matrix products, arithmetic and copies ran while one was open for 0% of the time, Pallas kernels for 27%

profile of v2, /device:TPU:0, one launch (start us, length us, event | category | flops | bytes accessed | tf_op | source)
XLA Modules:
  0.0 45.7 jit_solution(2788515977080675253)
XLA Ops:
  0.5 1.5 %pack_own.1 = (bf16[2,8,4992]{2,1,0:T(8,128)(2,1)S(1)}, bf16[2,8,4992]{2,1,0:T(8,128)(2,1)S(1)}, bf16[2,8,4992]{2,1,0:T(8,128)(2,1)S(1)}) custom-call(s32[1]{0:T(128)} %bitcast.me_ref.other_ref.after_ref, s32[1]{0:T(128)} %bitcast.1.slab_ref, bf16[8,160000]{1,0:T(8,128)(2,1)} %bitcast.10, s32[1]{0:T(128)} %bitcast.me_ref.other_ref.after_ref, ...), custom_call_target="tpu_custom_call" | custom-call | bytes 1277952 | tf_op jit(solution)/shard_map/pack_own/pallas_call | solution.py:86
  2.0 2.5 %collective-permute-start.1 = (bf16[2,8,4992]{2,1,0:T(8,128)(2,1)S(1)}, bf16[2,8,4992]{2,1,0:T(8,128)(2,1)S(1)}, u32[]{:S(2)}, u32[]{:S(2)}) collective-permute-start(bf16[2,8,4992]{2,1,0:T(8,128)(2,1)S(1)} %get-tuple-element.27), channel_id=1, source_target_pairs={{0,8},{4,12},{8,0},{12,4},{16,24},{20,28},{24,16},{28,20},{1,9},{5... | collective-permute-start | bytes 479240 | tf_op jit(solution)/shard_map/ppermute | solution.py:433
  4.4 1.5 %collective-permute-start.2 = (bf16[2,8,4992]{2,1,0:T(8,128)(2,1)S(1)}, bf16[2,8,4992]{2,1,0:T(8,128)(2,1)S(1)}, u32[]{:S(2)}, u32[]{:S(2)}) collective-permute-start(bf16[2,8,4992]{2,1,0:T(8,128)(2,1)S(1)} %get-tuple-element.28), channel_id=1, source_target_pairs={{0,16},{4,20},{8,24},{12,28},{16,0},{20,4},{24,8},{28,12},{1,17},{... | collective-permute-start | bytes 479240 | tf_op jit(solution)/shard_map/ppermute | solution.py:433
  6.0 1.8 %pack_rest.1 = (bf16[2,8,10016]{2,1,0:T(8,128)(2,1)S(1)}, bf16[2,8,10016]{2,1,0:T(8,128)(2,1)S(1)}, bf16[2,8,10016]{2,1,0:T(8,128)(2,1)S(1)}) custom-call(s32[1]{0:T(128)} %bitcast.me_ref.other_ref.after_ref, s32[1]{0:T(128)} %bitcast.1.slab_ref, bf16[8,160000]{1,0:T(8,128)(2,1)} %bitcast.11, bf16[8,160000]{1,0:T(8,128)(2,1)S(1)} %collective-permute-done.other_ref, ...), custom_call_target="tpu_custom_call" | custom-call | bytes 2564096 | tf_op jit(solution)/shard_map/pack_rest/pallas_call | solution.py:86
  7.8 2.0 %collective-permute-start.5 = (bf16[2,8,10016]{2,1,0:T(8,128)(2,1)S(1)}, bf16[2,8,10016]{2,1,0:T(8,128)(2,1)S(1)}, u32[]{:S(2)}, u32[]{:S(2)}) collective-permute-start(bf16[2,8,10016]{2,1,0:T(8,128)(2,1)S(1)} %get-tuple-element.30), channel_id=1, source_target_pairs={{0,8},{4,12},{8,0},{12,4},{16,24},{20,28},{24,16},{28,20},{1,9},{5... | collective-permute-start | bytes 961544 | tf_op jit(solution)/shard_map/ppermute | solution.py:433
  9.8 1.3 %collective-permute-start.6 = (bf16[2,8,10016]{2,1,0:T(8,128)(2,1)S(1)}, bf16[2,8,10016]{2,1,0:T(8,128)(2,1)S(1)}, u32[]{:S(2)}, u32[]{:S(2)}) collective-permute-start(bf16[2,8,10016]{2,1,0:T(8,128)(2,1)S(1)} %get-tuple-element.31), channel_id=1, source_target_pairs={{0,16},{4,20},{8,24},{12,28},{16,0},{20,4},{24,8},{28,12},{1,17},{... | collective-permute-start | bytes 961544 | tf_op jit(solution)/shard_map/ppermute | solution.py:433
  11.2 1.1 %collective-permute-start.7 = (bf16[2,8,10016]{2,1,0:T(8,128)(2,1)S(1)}, bf16[2,8,10016]{2,1,0:T(8,128)(2,1)S(1)}, u32[]{:S(2)}, u32[]{:S(2)}) collective-permute-start(bf16[2,8,10016]{2,1,0:T(8,128)(2,1)S(1)} %get-tuple-element.26.after_ref), channel_id=1, source_target_pairs={{0,24},{4,28},{8,16},{12,20},{16,8},{20,12},{24,0},{28,4},{1,25},{... | collective-permute-start | bytes 961544 | tf_op jit(solution)/shard_map/ppermute | solution.py:433
  12.3 1.2 %pack_all.1.refs_3_.home_ref = bf16[2,8,20000]{2,1,0:T(8,128)(2,1)S(1)} custom-call(s32[1]{0:T(128)} %bitcast.me_ref.other_ref.after_ref, s32[1]{0:T(128)} %bitcast.1.slab_ref, bf16[8,160000]{1,0:T(8,128)(2,1)} %bitcast.12, bf16[8,160000]{1,0:T(8,128)(2,1)S(1)} %collective-permute-done.other_ref, bf16[2,8,10016]{2,1,0:T(8,128)(2,1)S(1)} %get-tuple-element.26.after_ref), custom_call_target="tpu_custom_call" | custom-call | bytes 1280000 | tf_op jit(solution)/shard_map/pack_all/pallas_call | solution.py:86
  14.5 1.5 %collective-permute-done.4.refs_3_ = bf16[3,8,4992]{2,1,0:T(8,128)(2,1)S(1)} collective-permute-done((bf16[3,8,4992]{2,1,0:T(8,128)(2,1)S(1)}, bf16[3,8,4992]{2,1,0:T(8,128)(2,1)S(1)}, u32[]{:S(2)}, u32[]{:S(2)}) %collective-permute-start.4) | collective-permute-done | bytes 239648 | tf_op jit(solution)/shard_map/ppermute | solution.py:433
  16.0 1.6 %collective-permute-start.8 = (bf16[3,2,8,4992]{3,2,1,0:T(8,128)(2,1)S(1)}, bf16[3,2,8,4992]{3,2,1,0:T(8,128)(2,1)S(1)}, u32[]{:S(2)}, u32[]{:S(2)}) collective-permute-start(bf16[3,2,8,4992]{3,2,1,0:T(8,128)(2,1)S(1)} %join.1.refs_0_), channel_id=1, source_target_pairs={{0,1},{1,0},{2,3},{3,2},{4,5},{5,4},{6,7},{7,6},{8,9},{9,8},{10,11... | collective-permute-start | bytes 1437704 | tf_op jit(solution)/shard_map/ppermute | solution.py:433
  17.6 6.2 %mask_integrals.1 = (bf16[50,400,256]{2,1,0:T(8,128)(2,1)S(1)}, bf16[256,256]{1,0:T(8,128)(2,1)S(1)}, bf16[256,256]{1,0:T(8,128)(2,1)S(1)}, f32[8,256]{1,0:T(8,128)S(1)}) custom-call(s32[1]{0:T(128)} %bitcast.me_ref.other_ref.after_ref, s32[1]{0:T(128)} %bitcast.1.slab_ref, s32[400]{0:T(512)} %irrep_ref.1, f32[8]{0:T(128)} %occ_ref.1, f32[32]{0:T(128)} %virt_ref.1, ...), custom_call_target="tpu_custom_call" | custom-call | tf_op jit(solution)/shard_map/mask_integrals/pallas_call | solution.py:179
  23.8 0.6 %contract.2.refs_4_ = f32[64,256]{1,0:T(8,128)S(1)} custom-call(s32[1]{0:T(128)} %bitcast.1.slab_ref, s32[1]{0:T(128)} %bitcast.me_ref.other_ref.after_ref, bf16[2,8,20000]{2,1,0:T(8,128)(2,1)S(1)} %pack_all.1.refs_3_.home_ref, bf16[20000,256]{1,0:T(8,128)(2,1)S(1)} %bitcast.7, bf16[3,2,8,4992]{3,2,1,0:T(8,128)(2,1)S(1)} %join.1.refs_0_), custom_call_target="tpu_custom_call" | custom-call | flops 163577856 | bytes 3194880 | tf_op jit(solution)/shard_map/contract/pallas_call | solution.py:362
  24.4 3.5 %collective-permute-done.6.refs_1_ = bf16[2,8,10016]{2,1,0:T(8,128)(2,1)S(1)} collective-permute-done((bf16[2,8,10016]{2,1,0:T(8,128)(2,1)S(1)}, bf16[2,8,10016]{2,1,0:T(8,128)(2,1)S(1)}, u32[]{:S(2)}, u32[]{:S(2)}) %collective-permute-start.6) | collective-permute-done | bytes 320544 | tf_op jit(solution)/shard_map/ppermute | solution.py:433
  28.0 1.1 %collective-permute-done.8.refs_3_ = bf16[3,2,8,4992]{3,2,1,0:T(8,128)(2,1)S(1)} collective-permute-done((bf16[3,2,8,4992]{3,2,1,0:T(8,128)(2,1)S(1)}, bf16[3,2,8,4992]{3,2,1,0:T(8,128)(2,1)S(1)}, u32[]{:S(2)}, u32[]{:S(2)}) %collective-permute-start.8) | collective-permute-done | bytes 479264 | tf_op jit(solution)/shard_map/ppermute | solution.py:433
  29.0 1.5 %contract.3 = (f32[4,8,256]{2,1,0:T(8,128)S(1)}, f32[4,8,256]{2,1,0:T(8,128)S(1)}, f32[64,256]{1,0:T(8,128)S(1)}) custom-call(s32[1]{0:T(128)} %bitcast.1.slab_ref, s32[1]{0:T(128)} %bitcast.me_ref.other_ref.after_ref, bf16[2,8,20000]{2,1,0:T(8,128)(2,1)S(1)} %pack_all.1.refs_3_.home_ref, bf16[20000,256]{1,0:T(8,128)(2,1)S(1)} %bitcast.8, ...), custom_call_target="tpu_custom_call" | custom-call | flops 328204288 | bytes 6410240 | tf_op jit(solution)/shard_map/contract/pallas_call | solution.py:362
  30.6 1.0 %mirror_blocks.1.refs_0_ = f32[32,4,128]{2,1,0:T(4,128)} custom-call(s32[1]{0:T(128)} %bitcast.me_ref.other_ref.after_ref, f32[64,256]{1,0:T(8,128)S(1)} %get-tuple-element.36.total_ref, bf16[256,256]{1,0:T(8,128)(2,1)S(1)} %get-tuple-element.37.select_ref), custom_call_target="tpu_custom_call" | custom-call | flops 25165824 | bytes 131072 | tf_op jit(solution)/shard_map/mirror_blocks/pallas_call | solution.py:337
  31.8 5.4 %all-to-all-start = ((f32[32,4,128]{2,1,0:T(4,128)}), f32[32,4,128]{2,1,0:T(4,128)S(1)}, u32[]{:S(2)}, u32[]{:S(2)}) async-start(f32[32,4,128]{2,1,0:T(4,128)} %tie.3), calls=%async_computation | async-start | bytes 131072 | tf_op jit(solution)/shard_map/all_to_all | solution.py:471
  37.2 2.7 %collective-permute-start.10 = (f32[8,256]{1,0:T(8,128)S(1)}, f32[8,256]{1,0:T(8,128)S(1)}, u32[]{:S(2)}, u32[]{:S(2)}) collective-permute-start(f32[8,256]{1,0:T(8,128)S(1)} %get-tuple-element.42), channel_id=1, source_target_pairs={{0,24},{4,28},{8,16},{12,20},{16,8},{20,12},{24,0},{28,4},{1,25},{... | collective-permute-start | bytes 24584 | tf_op jit(solution)/shard_map/ppermute | solution.py:433
  40.0 0.6 %collective-permute-start.11 = (f32[8,256]{1,0:T(8,128)S(1)}, f32[8,256]{1,0:T(8,128)S(1)}, u32[]{:S(2)}, u32[]{:S(2)}) collective-permute-start(f32[8,256]{1,0:T(8,128)S(1)} %get-tuple-element.43), channel_id=1, source_target_pairs={{0,16},{4,20},{8,24},{12,28},{16,0},{20,4},{24,8},{28,12},{1,17},{... | collective-permute-start | bytes 24584 | tf_op jit(solution)/shard_map/ppermute | solution.py:433
  40.8 1.1 %collective-permute-done.10.refs_1_ = f32[8,256]{1,0:T(8,128)S(1)} collective-permute-done((f32[8,256]{1,0:T(8,128)S(1)}, f32[8,256]{1,0:T(8,128)S(1)}, u32[]{:S(2)}, u32[]{:S(2)}) %collective-permute-start.10) | collective-permute-done | bytes 8224 | tf_op jit(solution)/shard_map/ppermute | solution.py:433
  41.8 1.8 %collective-permute-done.11.refs_2_ = f32[8,256]{1,0:T(8,128)S(1)} collective-permute-done((f32[8,256]{1,0:T(8,128)S(1)}, f32[8,256]{1,0:T(8,128)S(1)}, u32[]{:S(2)}, u32[]{:S(2)}) %collective-permute-start.11) | collective-permute-done | bytes 8224 | tf_op jit(solution)/shard_map/ppermute | solution.py:433
  43.7 0.5 %collective-permute-done.12.refs_3_ = f32[8,256]{1,0:T(8,128)S(1)} collective-permute-done((f32[8,256]{1,0:T(8,128)S(1)}, f32[8,256]{1,0:T(8,128)S(1)}, u32[]{:S(2)}, u32[]{:S(2)}) %collective-permute-start.12) | collective-permute-done | bytes 8224 | tf_op jit(solution)/shard_map/ppermute | solution.py:433
  44.2 0.5 %all-to-all-done.mirror_ref = f32[32,4,128]{2,1,0:T(4,128)S(1)} async-done(((f32[32,4,128]{2,1,0:T(4,128)}), f32[32,4,128]{2,1,0:T(4,128)S(1)}, u32[]{:S(2)}, u32[]{:S(2)}) %all-to-all-start) | async-done | bytes 65568 | tf_op jit(solution)/shard_map/all_to_all | solution.py:471
  44.7 1.0 %finish.1 = f32[8,8,32]{2,1,0:T(8,128)} custom-call(f32[32,4,128]{2,1,0:T(4,128)S(1)} %all-to-all-done.mirror_ref, f32[8,256]{1,0:T(8,128)S(1)} %get-tuple-element.32.refs_3_.denominator_ref, bf16[256,256]{1,0:T(8,128)(2,1)S(1)} %get-tuple-element.39.select_ref, f32[8,256]{1,0:T(8,128)S(1)} %get-tuple-element.41.refs_0_, ...), custom_call_target="tpu_custom_call" | custom-call | flops 3145728 | bytes 131072 | tf_op jit(solution)/shard_map/finish/pallas_call | solution.py:421
  (17 shorter events, 2.0 us)
Async XLA Ops:
  0.0 6.0 %collective-permute-start = (bf16[8,160000]{1,0:T(8,128)(2,1)}, bf16[8,160000]{1,0:T(8,128)(2,1)S(1)}, u32[]{:S(2)}, u32[]{:S(2)}) collective-permute-start(bf16[8,160000]{1,0:T(8,128)(2,1)} %bitcast.9), channel_id=1, source_target_pairs={{0,4},{4,0},{8,12},{12,8},{16,20},{20,16},{24,28},{28,24},{1,5},{5... | collective-permute-start | bytes 7680008 | tf_op jit(solution)/shard_map/ppermute | solution.py:433
  2.0 9.2 %collective-permute-start.1 = (bf16[2,8,4992]{2,1,0:T(8,128)(2,1)S(1)}, bf16[2,8,4992]{2,1,0:T(8,128)(2,1)S(1)}, u32[]{:S(2)}, u32[]{:S(2)}) collective-permute-start(bf16[2,8,4992]{2,1,0:T(8,128)(2,1)S(1)} %get-tuple-element.27), channel_id=1, source_target_pairs={{0,8},{4,12},{8,0},{12,4},{16,24},{20,28},{24,16},{28,20},{1,9},{5... | collective-permute-start | bytes 479240 | tf_op jit(solution)/shard_map/ppermute | solution.py:433
  4.4 9.5 %collective-permute-start.2 = (bf16[2,8,4992]{2,1,0:T(8,128)(2,1)S(1)}, bf16[2,8,4992]{2,1,0:T(8,128)(2,1)S(1)}, u32[]{:S(2)}, u32[]{:S(2)}) collective-permute-start(bf16[2,8,4992]{2,1,0:T(8,128)(2,1)S(1)} %get-tuple-element.28), channel_id=1, source_target_pairs={{0,16},{4,20},{8,24},{12,28},{16,0},{20,4},{24,8},{28,12},{1,17},{... | collective-permute-start | bytes 479240 | tf_op jit(solution)/shard_map/ppermute | solution.py:433
  6.0 8.4 %collective-permute-start.3 = (bf16[2,8,4992]{2,1,0:T(8,128)(2,1)S(1)}, bf16[2,8,4992]{2,1,0:T(8,128)(2,1)S(1)}, u32[]{:S(2)}, u32[]{:S(2)}) collective-permute-start(bf16[2,8,4992]{2,1,0:T(8,128)(2,1)S(1)} %get-tuple-element.25.after_ref), channel_id=1, source_target_pairs={{0,24},{4,28},{8,16},{12,20},{16,8},{20,12},{24,0},{28,4},{1,25},{... | collective-permute-start | bytes 479240 | tf_op jit(solution)/shard_map/ppermute | solution.py:433
  7.8 16.6 %collective-permute-start.5 = (bf16[2,8,10016]{2,1,0:T(8,128)(2,1)S(1)}, bf16[2,8,10016]{2,1,0:T(8,128)(2,1)S(1)}, u32[]{:S(2)}, u32[]{:S(2)}) collective-permute-start(bf16[2,8,10016]{2,1,0:T(8,128)(2,1)S(1)} %get-tuple-element.30), channel_id=1, source_target_pairs={{0,8},{4,12},{8,0},{12,4},{16,24},{20,28},{24,16},{28,20},{1,9},{5... | collective-permute-start | bytes 961544 | tf_op jit(solution)/shard_map/ppermute | solution.py:433
  9.8 18.1 %collective-permute-start.6 = (bf16[2,8,10016]{2,1,0:T(8,128)(2,1)S(1)}, bf16[2,8,10016]{2,1,0:T(8,128)(2,1)S(1)}, u32[]{:S(2)}, u32[]{:S(2)}) collective-permute-start(bf16[2,8,10016]{2,1,0:T(8,128)(2,1)S(1)} %get-tuple-element.31), channel_id=1, source_target_pairs={{0,16},{4,20},{8,24},{12,28},{16,0},{20,4},{24,8},{28,12},{1,17},{... | collective-permute-start | bytes 961544 | tf_op jit(solution)/shard_map/ppermute | solution.py:433
  11.2 16.8 %collective-permute-start.7 = (bf16[2,8,10016]{2,1,0:T(8,128)(2,1)S(1)}, bf16[2,8,10016]{2,1,0:T(8,128)(2,1)S(1)}, u32[]{:S(2)}, u32[]{:S(2)}) collective-permute-start(bf16[2,8,10016]{2,1,0:T(8,128)(2,1)S(1)} %get-tuple-element.26.after_ref), channel_id=1, source_target_pairs={{0,24},{4,28},{8,16},{12,20},{16,8},{20,12},{24,0},{28,4},{1,25},{... | collective-permute-start | bytes 961544 | tf_op jit(solution)/shard_map/ppermute | solution.py:433
  14.4 1.6 %collective-permute-start.4 = (bf16[3,8,4992]{2,1,0:T(8,128)(2,1)S(1)}, bf16[3,8,4992]{2,1,0:T(8,128)(2,1)S(1)}, u32[]{:S(2)}, u32[]{:S(2)}) collective-permute-start(bf16[3,8,4992]{2,1,0:T(8,128)(2,1)S(1)} %take_other.1), channel_id=1, source_target_pairs={{0,4},{4,0},{8,12},{12,8},{16,20},{20,16},{24,28},{28,24},{1,5},{5... | collective-permute-start | bytes 718856 | tf_op jit(solution)/shard_map/ppermute | solution.py:433
  16.0 13.1 %collective-permute-start.8 = (bf16[3,2,8,4992]{3,2,1,0:T(8,128)(2,1)S(1)}, bf16[3,2,8,4992]{3,2,1,0:T(8,128)(2,1)S(1)}, u32[]{:S(2)}, u32[]{:S(2)}) collective-permute-start(bf16[3,2,8,4992]{3,2,1,0:T(8,128)(2,1)S(1)} %join.1.refs_0_), channel_id=1, source_target_pairs={{0,1},{1,0},{2,3},{3,2},{4,5},{5,4},{6,7},{7,6},{8,9},{9,8},{10,11... | collective-permute-start | bytes 1437704 | tf_op jit(solution)/shard_map/ppermute | solution.py:433
  30.6 1.3 %collective-permute-start.9 = (f32[4,8,256]{2,1,0:T(8,128)S(1)}, f32[4,8,256]{2,1,0:T(8,128)S(1)}, u32[]{:S(2)}, u32[]{:S(2)}) collective-permute-start(f32[4,8,256]{2,1,0:T(8,128)S(1)} %get-tuple-element.38), channel_id=1, source_target_pairs={{0,4},{4,0},{8,12},{12,8},{16,20},{20,16},{24,28},{28,24},{1,5},{5... | collective-permute-start | bytes 98312 | tf_op jit(solution)/shard_map/ppermute | solution.py:433
  31.8 12.9 %all-to-all-start = ((f32[32,4,128]{2,1,0:T(4,128)}), f32[32,4,128]{2,1,0:T(4,128)S(1)}, u32[]{:S(2)}, u32[]{:S(2)}) async-start(f32[32,4,128]{2,1,0:T(4,128)} %tie.3), calls=%async_computation | async-start | bytes 131072 | tf_op jit(solution)/shard_map/all_to_all | solution.py:471
  37.2 4.6 %collective-permute-start.10 = (f32[8,256]{1,0:T(8,128)S(1)}, f32[8,256]{1,0:T(8,128)S(1)}, u32[]{:S(2)}, u32[]{:S(2)}) collective-permute-start(f32[8,256]{1,0:T(8,128)S(1)} %get-tuple-element.42), channel_id=1, source_target_pairs={{0,24},{4,28},{8,16},{12,20},{16,8},{20,12},{24,0},{28,4},{1,25},{... | collective-permute-start | bytes 24584 | tf_op jit(solution)/shard_map/ppermute | solution.py:433
  40.0 3.7 %collective-permute-start.11 = (f32[8,256]{1,0:T(8,128)S(1)}, f32[8,256]{1,0:T(8,128)S(1)}, u32[]{:S(2)}, u32[]{:S(2)}) collective-permute-start(f32[8,256]{1,0:T(8,128)S(1)} %get-tuple-element.43), channel_id=1, source_target_pairs={{0,16},{4,20},{8,24},{12,28},{16,0},{20,4},{24,8},{28,12},{1,17},{... | collective-permute-start | bytes 24584 | tf_op jit(solution)/shard_map/ppermute | solution.py:433
  40.5 3.7 %collective-permute-start.12 = (f32[8,256]{1,0:T(8,128)S(1)}, f32[8,256]{1,0:T(8,128)S(1)}, u32[]{:S(2)}, u32[]{:S(2)}) collective-permute-start(f32[8,256]{1,0:T(8,128)S(1)} %get-tuple-element.44), channel_id=1, source_target_pairs={{0,8},{4,12},{8,0},{12,4},{16,24},{20,28},{24,16},{28,20},{1,9},{5... | collective-permute-start | bytes 24584 | tf_op jit(solution)/shard_map/ppermute | solution.py:433

commit v3 on v1

--- a/solution.py
+++ b/solution.py
@@ -10,7 +10,7 @@
 
 IRREPS = 8
 MIB = 2**20
-SHARE = 0.25
+SHARE = 0.245
 TIE_FLOPS = 10**10
 
 

time: 45.1 us -> 44.9 us (level)
  starting transfers between devices: 19.8 us -> 19.3 us
where the time goes in v3:
time: 44.9 us; the launch traced here: 44.6 us
  starting transfers between devices  19.3 us (43%)
  Pallas kernels  15 us (33%)
  waiting for transfers between devices  10.2 us (23%)
    ppermute x13, starting transfers between devices, swap(): lax.ppermute(values, axis, [(p, p ^ bits) for p in range(lax.axis_size(ax...  14.3 us
    ppermute x13, waiting for transfers between devices, swap(): lax.ppermute(values, axis, [(p, p ^ bits) for p in range(lax.axis_size(ax...  9.68 us
    pallas_call x1, Pallas kernels, mask(): pl.pallas_call(functools.partial(mask_kernel, per_step, parts), grid=(chu...  6.24 us
    all_to_all x1, starting transfers between devices, local(): lax.all_to_all(mirror, ('pair', 'slab'), split_axis=0, concat_axis=0, til...  4.96 us
    pallas_call x3, Pallas kernels, pack(): pl.pallas_call(functools.partial(pack_kernel, rows_local, shared, which),...  4.49 us
    pallas_call x3, Pallas kernels, contract(): pl.pallas_call(functools.partial(contract_kernel, which, shared), out_sha...  2.18 us
    pallas_call x1, Pallas kernels, finish(): pl.pallas_call(finish_kernel, out_shape=jax.ShapeDtypeStruct((rows, first...  1.04 us
    pallas_call x1, Pallas kernels, mirror_blocks(): pl.pallas_call(mirror_kernel, out_shape=jax.ShapeDtypeStruct((count * sla...  1.01 us
  transfers between devices with their start and end apart: 14, of which 9 were waited for; matrix products, arithmetic and copies ran while one was open for 0% of the time, Pallas kernels for 30%

profile of v3, /device:TPU:0, one launch (start us, length us, event | category | flops | bytes accessed | tf_op | source)
XLA Modules:
  0.0 44.6 jit_solution(9000541777253957852)
XLA Ops:
  0.5 1.5 %pack_own.1 = (bf16[2,8,4864]{2,1,0:T(8,128)(2,1)S(1)}, bf16[2,8,4864]{2,1,0:T(8,128)(2,1)S(1)}, bf16[2,8,4864]{2,1,0:T(8,128)(2,1)S(1)}) custom-call(s32[1]{0:T(128)} %bitcast.me_ref.other_ref.after_ref, s32[1]{0:T(128)} %bitcast.1.slab_ref, bf16[8,160000]{1,0:T(8,128)(2,1)} %bitcast.11, s32[1]{0:T(128)} %bitcast.me_ref.other_ref.after_ref, ...), custom_call_target="tpu_custom_call" | custom-call | bytes 1245184 | tf_op jit(solution)/shard_map/pack_own/pallas_call | solution.py:86
  2.0 2.5 %collective-permute-start.1 = (bf16[2,8,4864]{2,1,0:T(8,128)(2,1)S(1)}, bf16[2,8,4864]{2,1,0:T(8,128)(2,1)S(1)}, u32[]{:S(2)}, u32[]{:S(2)}) collective-permute-start(bf16[2,8,4864]{2,1,0:T(8,128)(2,1)S(1)} %get-tuple-element.27), channel_id=1, source_target_pairs={{0,8},{4,12},{8,0},{12,4},{16,24},{20,28},{24,16},{28,20},{1,9},{5... | collective-permute-start | bytes 466952 | tf_op jit(solution)/shard_map/ppermute | solution.py:433
  4.4 1.5 %collective-permute-start.2 = (bf16[2,8,4864]{2,1,0:T(8,128)(2,1)S(1)}, bf16[2,8,4864]{2,1,0:T(8,128)(2,1)S(1)}, u32[]{:S(2)}, u32[]{:S(2)}) collective-permute-start(bf16[2,8,4864]{2,1,0:T(8,128)(2,1)S(1)} %get-tuple-element.28), channel_id=1, source_target_pairs={{0,16},{4,20},{8,24},{12,28},{16,0},{20,4},{24,8},{28,12},{1,17},{... | collective-permute-start | bytes 466952 | tf_op jit(solution)/shard_map/ppermute | solution.py:433
  6.0 1.8 %pack_rest.1 = (bf16[2,8,10272]{2,1,0:T(8,128)(2,1)S(1)}, bf16[2,8,10272]{2,1,0:T(8,128)(2,1)S(1)}, bf16[2,8,10272]{2,1,0:T(8,128)(2,1)S(1)}) custom-call(s32[1]{0:T(128)} %bitcast.me_ref.other_ref.after_ref, s32[1]{0:T(128)} %bitcast.1.slab_ref, bf16[8,160000]{1,0:T(8,128)(2,1)} %bitcast.12, bf16[8,160000]{1,0:T(8,128)(2,1)S(1)} %collective-permute-done.other_ref, ...), custom_call_target="tpu_custom_call" | custom-call | bytes 2629632 | tf_op jit(solution)/shard_map/pack_rest/pallas_call | solution.py:86
  7.8 2.0 %collective-permute-start.6 = (bf16[2,8,10272]{2,1,0:T(8,128)(2,1)S(1)}, bf16[2,8,10272]{2,1,0:T(8,128)(2,1)S(1)}, u32[]{:S(2)}, u32[]{:S(2)}) collective-permute-start(bf16[2,8,10272]{2,1,0:T(8,128)(2,1)S(1)} %get-tuple-element.30), channel_id=1, source_target_pairs={{0,8},{4,12},{8,0},{12,4},{16,24},{20,28},{24,16},{28,20},{1,9},{5... | collective-permute-start | bytes 986120 | tf_op jit(solution)/shard_map/ppermute | solution.py:433
  9.9 1.3 %collective-permute-start.7 = (bf16[2,8,10272]{2,1,0:T(8,128)(2,1)S(1)}, bf16[2,8,10272]{2,1,0:T(8,128)(2,1)S(1)}, u32[]{:S(2)}, u32[]{:S(2)}) collective-permute-start(bf16[2,8,10272]{2,1,0:T(8,128)(2,1)S(1)} %get-tuple-element.31), channel_id=1, source_target_pairs={{0,16},{4,20},{8,24},{12,28},{16,0},{20,4},{24,8},{28,12},{1,17},{... | collective-permute-start | bytes 986120 | tf_op jit(solution)/shard_map/ppermute | solution.py:433
  11.2 1.0 %collective-permute-start.8 = (bf16[2,8,10272]{2,1,0:T(8,128)(2,1)S(1)}, bf16[2,8,10272]{2,1,0:T(8,128)(2,1)S(1)}, u32[]{:S(2)}, u32[]{:S(2)}) collective-permute-start(bf16[2,8,10272]{2,1,0:T(8,128)(2,1)S(1)} %get-tuple-element.26.after_ref), channel_id=1, source_target_pairs={{0,24},{4,28},{8,16},{12,20},{16,8},{20,12},{24,0},{28,4},{1,25},{... | collective-permute-start | bytes 986120 | tf_op jit(solution)/shard_map/ppermute | solution.py:433
  12.2 1.2 %pack_all.1.refs_3_.home_ref = bf16[2,8,20000]{2,1,0:T(8,128)(2,1)S(1)} custom-call(s32[1]{0:T(128)} %bitcast.me_ref.other_ref.after_ref, s32[1]{0:T(128)} %bitcast.1.slab_ref, bf16[8,160000]{1,0:T(8,128)(2,1)} %bitcast.13, bf16[8,160000]{1,0:T(8,128)(2,1)S(1)} %collective-permute-done.other_ref, bf16[2,8,10272]{2,1,0:T(8,128)(2,1)S(1)} %get-tuple-element.26.after_ref), custom_call_target="tpu_custom_call" | custom-call | bytes 1280000 | tf_op jit(solution)/shard_map/pack_all/pallas_call | solution.py:86
  14.3 1.5 %collective-permute-done.4.refs_3_ = bf16[3,8,4864]{2,1,0:T(8,128)(2,1)S(1)} collective-permute-done((bf16[3,8,4864]{2,1,0:T(8,128)(2,1)S(1)}, bf16[3,8,4864]{2,1,0:T(8,128)(2,1)S(1)}, u32[]{:S(2)}, u32[]{:S(2)}) %collective-permute-start.4) | collective-permute-done | bytes 233504 | tf_op jit(solution)/shard_map/ppermute | solution.py:433
  15.8 1.6 %collective-permute-start.5 = (bf16[3,2,8,4864]{3,2,1,0:T(8,128)(2,1)S(1)}, bf16[3,2,8,4864]{3,2,1,0:T(8,128)(2,1)S(1)}, u32[]{:S(2)}, u32[]{:S(2)}) collective-permute-start(bf16[3,2,8,4864]{3,2,1,0:T(8,128)(2,1)S(1)} %join.1.refs_0_), channel_id=1, source_target_pairs={{0,1},{1,0},{2,3},{3,2},{4,5},{5,4},{6,7},{7,6},{8,9},{9,8},{10,11... | collective-permute-start | bytes 1400840 | tf_op jit(solution)/shard_map/ppermute | solution.py:433
  17.4 6.2 %mask_integrals.1 = (bf16[50,400,256]{2,1,0:T(8,128)(2,1)S(1)}, bf16[256,256]{1,0:T(8,128)(2,1)S(1)}, bf16[256,256]{1,0:T(8,128)(2,1)S(1)}, f32[8,256]{1,0:T(8,128)S(1)}) custom-call(s32[1]{0:T(128)} %bitcast.me_ref.other_ref.after_ref, s32[1]{0:T(128)} %bitcast.1.slab_ref, s32[400]{0:T(512)} %irrep_ref.1, f32[8]{0:T(128)} %occ_ref.1, f32[32]{0:T(128)} %virt_ref.1, ...), custom_call_target="tpu_custom_call" | custom-call | tf_op jit(solution)/shard_map/mask_integrals/pallas_call | solution.py:179
  23.7 0.6 %contract.3.refs_3_ = f32[64,256]{1,0:T(8,128)S(1)} custom-call(s32[1]{0:T(128)} %bitcast.1.slab_ref, s32[1]{0:T(128)} %bitcast.me_ref.other_ref.after_ref, bf16[2,8,20000]{2,1,0:T(8,128)(2,1)S(1)} %pack_all.1.refs_3_.home_ref, bf16[20000,256]{1,0:T(8,128)(2,1)S(1)} %bitcast.7, bf16[3,2,8,4864]{3,2,1,0:T(8,128)(2,1)S(1)} %join.1.refs_0_), custom_call_target="tpu_custom_call" | custom-call | flops 159383552 | bytes 3112960 | tf_op jit(solution)/shard_map/contract/pallas_call | solution.py:362
  24.3 3.9 %collective-permute-done.7.refs_1_ = bf16[2,8,10272]{2,1,0:T(8,128)(2,1)S(1)} collective-permute-done((bf16[2,8,10272]{2,1,0:T(8,128)(2,1)S(1)}, bf16[2,8,10272]{2,1,0:T(8,128)(2,1)S(1)}, u32[]{:S(2)}, u32[]{:S(2)}) %collective-permute-start.7) | collective-permute-done | bytes 328736 | tf_op jit(solution)/shard_map/ppermute | solution.py:433
  28.2 1.1 %contract.4.refs_1_ = f32[64,256]{1,0:T(8,128)S(1)} custom-call(s32[1]{0:T(128)} %bitcast.1.slab_ref, s32[1]{0:T(128)} %bitcast.me_ref.other_ref.after_ref, bf16[2,8,20000]{2,1,0:T(8,128)(2,1)S(1)} %pack_all.1.refs_3_.home_ref, bf16[20000,256]{1,0:T(8,128)(2,1)S(1)} %bitcast.8, bf16[2,8,10272]{2,1,0:T(8,128)(2,1)S(1)} %get-tuple-element.33.refs_0_, ...), custom_call_target="tpu_custom_call" | custom-call | flops 336592896 | bytes 6574080 | tf_op jit(solution)/shard_map/contract/pallas_call | solution.py:362
  29.2 0.6 %contract.5 = (f32[4,8,256]{2,1,0:T(8,128)S(1)}, f32[4,8,256]{2,1,0:T(8,128)S(1)}, f32[64,256]{1,0:T(8,128)S(1)}) custom-call(s32[1]{0:T(128)} %bitcast.1.slab_ref, s32[1]{0:T(128)} %bitcast.me_ref.other_ref.after_ref, bf16[2,8,20000]{2,1,0:T(8,128)(2,1)S(1)} %pack_all.1.refs_3_.home_ref, bf16[20000,256]{1,0:T(8,128)(2,1)S(1)} %bitcast.9, ...), custom_call_target="tpu_custom_call" | custom-call | flops 159383552 | bytes 3112960 | tf_op jit(solution)/shard_map/contract/pallas_call | solution.py:362
  30.0 1.0 %mirror_blocks.1.refs_0_ = f32[32,4,128]{2,1,0:T(4,128)} custom-call(s32[1]{0:T(128)} %bitcast.me_ref.other_ref.after_ref, f32[64,256]{1,0:T(8,128)S(1)} %get-tuple-element.36.total_ref, bf16[256,256]{1,0:T(8,128)(2,1)S(1)} %get-tuple-element.37.select_ref), custom_call_target="tpu_custom_call" | custom-call | flops 25165824 | bytes 131072 | tf_op jit(solution)/shard_map/mirror_blocks/pallas_call | solution.py:338
  31.1 5.0 %all-to-all-start = ((f32[32,4,128]{2,1,0:T(4,128)}), f32[32,4,128]{2,1,0:T(4,128)S(1)}, u32[]{:S(2)}, u32[]{:S(2)}) async-start(f32[32,4,128]{2,1,0:T(4,128)} %tie.3), calls=%async_computation | async-start | bytes 131072 | tf_op jit(solution)/shard_map/all_to_all | solution.py:472
  36.1 2.7 %collective-permute-start.10 = (f32[8,256]{1,0:T(8,128)S(1)}, f32[8,256]{1,0:T(8,128)S(1)}, u32[]{:S(2)}, u32[]{:S(2)}) collective-permute-start(f32[8,256]{1,0:T(8,128)S(1)} %get-tuple-element.42), channel_id=1, source_target_pairs={{0,24},{4,28},{8,16},{12,20},{16,8},{20,12},{24,0},{28,4},{1,25},{... | collective-permute-start | bytes 24584 | tf_op jit(solution)/shard_map/ppermute | solution.py:433
  38.8 0.6 %collective-permute-start.11 = (f32[8,256]{1,0:T(8,128)S(1)}, f32[8,256]{1,0:T(8,128)S(1)}, u32[]{:S(2)}, u32[]{:S(2)}) collective-permute-start(f32[8,256]{1,0:T(8,128)S(1)} %get-tuple-element.43), channel_id=1, source_target_pairs={{0,16},{4,20},{8,24},{12,28},{16,0},{20,4},{24,8},{28,12},{1,17},{... | collective-permute-start | bytes 24584 | tf_op jit(solution)/shard_map/ppermute | solution.py:433
  39.6 1.1 %collective-permute-done.10.refs_1_ = f32[8,256]{1,0:T(8,128)S(1)} collective-permute-done((f32[8,256]{1,0:T(8,128)S(1)}, f32[8,256]{1,0:T(8,128)S(1)}, u32[]{:S(2)}, u32[]{:S(2)}) %collective-permute-start.10) | collective-permute-done | bytes 8224 | tf_op jit(solution)/shard_map/ppermute | solution.py:433
  40.7 1.8 %collective-permute-done.11.refs_2_ = f32[8,256]{1,0:T(8,128)S(1)} collective-permute-done((f32[8,256]{1,0:T(8,128)S(1)}, f32[8,256]{1,0:T(8,128)S(1)}, u32[]{:S(2)}, u32[]{:S(2)}) %collective-permute-start.11) | collective-permute-done | bytes 8224 | tf_op jit(solution)/shard_map/ppermute | solution.py:433
  42.5 0.5 %collective-permute-done.12.refs_3_ = f32[8,256]{1,0:T(8,128)S(1)} collective-permute-done((f32[8,256]{1,0:T(8,128)S(1)}, f32[8,256]{1,0:T(8,128)S(1)}, u32[]{:S(2)}, u32[]{:S(2)}) %collective-permute-start.12) | collective-permute-done | bytes 8224 | tf_op jit(solution)/shard_map/ppermute | solution.py:433
  43.0 0.5 %all-to-all-done.mirror_ref = f32[32,4,128]{2,1,0:T(4,128)S(1)} async-done(((f32[32,4,128]{2,1,0:T(4,128)}), f32[32,4,128]{2,1,0:T(4,128)S(1)}, u32[]{:S(2)}, u32[]{:S(2)}) %all-to-all-start) | async-done | bytes 65568 | tf_op jit(solution)/shard_map/all_to_all | solution.py:472
  43.6 1.0 %finish.1 = f32[8,8,32]{2,1,0:T(8,128)} custom-call(f32[32,4,128]{2,1,0:T(4,128)S(1)} %all-to-all-done.mirror_ref, f32[8,256]{1,0:T(8,128)S(1)} %get-tuple-element.32.refs_3_.denominator_ref, bf16[256,256]{1,0:T(8,128)(2,1)S(1)} %get-tuple-element.39.select_ref, f32[8,256]{1,0:T(8,128)S(1)} %get-tuple-element.41.refs_0_, ...), custom_call_target="tpu_custom_call" | custom-call | flops 3145728 | bytes 131072 | tf_op jit(solution)/shard_map/finish/pallas_call | solution.py:421
  (18 shorter events, 2.0 us)
Async XLA Ops:
  0.0 6.0 %collective-permute-start = (bf16[8,160000]{1,0:T(8,128)(2,1)}, bf16[8,160000]{1,0:T(8,128)(2,1)S(1)}, u32[]{:S(2)}, u32[]{:S(2)}) collective-permute-start(bf16[8,160000]{1,0:T(8,128)(2,1)} %bitcast.10), channel_id=1, source_target_pairs={{0,4},{4,0},{8,12},{12,8},{16,20},{20,16},{24,28},{28,24},{1,5},{5... | collective-permute-start | bytes 7680008 | tf_op jit(solution)/shard_map/ppermute | solution.py:433
  2.0 9.2 %collective-permute-start.1 = (bf16[2,8,4864]{2,1,0:T(8,128)(2,1)S(1)}, bf16[2,8,4864]{2,1,0:T(8,128)(2,1)S(1)}, u32[]{:S(2)}, u32[]{:S(2)}) collective-permute-start(bf16[2,8,4864]{2,1,0:T(8,128)(2,1)S(1)} %get-tuple-element.27), channel_id=1, source_target_pairs={{0,8},{4,12},{8,0},{12,4},{16,24},{20,28},{24,16},{28,20},{1,9},{5... | collective-permute-start | bytes 466952 | tf_op jit(solution)/shard_map/ppermute | solution.py:433
  4.4 9.3 %collective-permute-start.2 = (bf16[2,8,4864]{2,1,0:T(8,128)(2,1)S(1)}, bf16[2,8,4864]{2,1,0:T(8,128)(2,1)S(1)}, u32[]{:S(2)}, u32[]{:S(2)}) collective-permute-start(bf16[2,8,4864]{2,1,0:T(8,128)(2,1)S(1)} %get-tuple-element.28), channel_id=1, source_target_pairs={{0,16},{4,20},{8,24},{12,28},{16,0},{20,4},{24,8},{28,12},{1,17},{... | collective-permute-start | bytes 466952 | tf_op jit(solution)/shard_map/ppermute | solution.py:433
  6.0 8.2 %collective-permute-start.3 = (bf16[2,8,4864]{2,1,0:T(8,128)(2,1)S(1)}, bf16[2,8,4864]{2,1,0:T(8,128)(2,1)S(1)}, u32[]{:S(2)}, u32[]{:S(2)}) collective-permute-start(bf16[2,8,4864]{2,1,0:T(8,128)(2,1)S(1)} %get-tuple-element.25.after_ref), channel_id=1, source_target_pairs={{0,24},{4,28},{8,16},{12,20},{16,8},{20,12},{24,0},{28,4},{1,25},{... | collective-permute-start | bytes 466952 | tf_op jit(solution)/shard_map/ppermute | solution.py:433
  7.8 16.4 %collective-permute-start.6 = (bf16[2,8,10272]{2,1,0:T(8,128)(2,1)S(1)}, bf16[2,8,10272]{2,1,0:T(8,128)(2,1)S(1)}, u32[]{:S(2)}, u32[]{:S(2)}) collective-permute-start(bf16[2,8,10272]{2,1,0:T(8,128)(2,1)S(1)} %get-tuple-element.30), channel_id=1, source_target_pairs={{0,8},{4,12},{8,0},{12,4},{16,24},{20,28},{24,16},{28,20},{1,9},{5... | collective-permute-start | bytes 986120 | tf_op jit(solution)/shard_map/ppermute | solution.py:433
  9.9 18.3 %collective-permute-start.7 = (bf16[2,8,10272]{2,1,0:T(8,128)(2,1)S(1)}, bf16[2,8,10272]{2,1,0:T(8,128)(2,1)S(1)}, u32[]{:S(2)}, u32[]{:S(2)}) collective-permute-start(bf16[2,8,10272]{2,1,0:T(8,128)(2,1)S(1)} %get-tuple-element.31), channel_id=1, source_target_pairs={{0,16},{4,20},{8,24},{12,28},{16,0},{20,4},{24,8},{28,12},{1,17},{... | collective-permute-start | bytes 986120 | tf_op jit(solution)/shard_map/ppermute | solution.py:433
  11.2 17.0 %collective-permute-start.8 = (bf16[2,8,10272]{2,1,0:T(8,128)(2,1)S(1)}, bf16[2,8,10272]{2,1,0:T(8,128)(2,1)S(1)}, u32[]{:S(2)}, u32[]{:S(2)}) collective-permute-start(bf16[2,8,10272]{2,1,0:T(8,128)(2,1)S(1)} %get-tuple-element.26.after_ref), channel_id=1, source_target_pairs={{0,24},{4,28},{8,16},{12,20},{16,8},{20,12},{24,0},{28,4},{1,25},{... | collective-permute-start | bytes 986120 | tf_op jit(solution)/shard_map/ppermute | solution.py:433
  14.2 1.6 %collective-permute-start.4 = (bf16[3,8,4864]{2,1,0:T(8,128)(2,1)S(1)}, bf16[3,8,4864]{2,1,0:T(8,128)(2,1)S(1)}, u32[]{:S(2)}, u32[]{:S(2)}) collective-permute-start(bf16[3,8,4864]{2,1,0:T(8,128)(2,1)S(1)} %take_other.1), channel_id=1, source_target_pairs={{0,4},{4,0},{8,12},{12,8},{16,20},{20,16},{24,28},{28,24},{1,5},{5... | collective-permute-start | bytes 700424 | tf_op jit(solution)/shard_map/ppermute | solution.py:433
  15.8 13.4 %collective-permute-start.5 = (bf16[3,2,8,4864]{3,2,1,0:T(8,128)(2,1)S(1)}, bf16[3,2,8,4864]{3,2,1,0:T(8,128)(2,1)S(1)}, u32[]{:S(2)}, u32[]{:S(2)}) collective-permute-start(bf16[3,2,8,4864]{3,2,1,0:T(8,128)(2,1)S(1)} %join.1.refs_0_), channel_id=1, source_target_pairs={{0,1},{1,0},{2,3},{3,2},{4,5},{5,4},{6,7},{7,6},{8,9},{9,8},{10,11... | collective-permute-start | bytes 1400840 | tf_op jit(solution)/shard_map/ppermute | solution.py:433
  29.8 1.3 %collective-permute-start.9 = (f32[4,8,256]{2,1,0:T(8,128)S(1)}, f32[4,8,256]{2,1,0:T(8,128)S(1)}, u32[]{:S(2)}, u32[]{:S(2)}) collective-permute-start(f32[4,8,256]{2,1,0:T(8,128)S(1)} %get-tuple-element.38), channel_id=1, source_target_pairs={{0,4},{4,0},{8,12},{12,8},{16,20},{20,16},{24,28},{28,24},{1,5},{5... | collective-permute-start | bytes 98312 | tf_op jit(solution)/shard_map/ppermute | solution.py:433
  31.1 12.5 %all-to-all-start = ((f32[32,4,128]{2,1,0:T(4,128)}), f32[32,4,128]{2,1,0:T(4,128)S(1)}, u32[]{:S(2)}, u32[]{:S(2)}) async-start(f32[32,4,128]{2,1,0:T(4,128)} %tie.3), calls=%async_computation | async-start | bytes 131072 | tf_op jit(solution)/shard_map/all_to_all | solution.py:472
  36.1 4.6 %collective-permute-start.10 = (f32[8,256]{1,0:T(8,128)S(1)}, f32[8,256]{1,0:T(8,128)S(1)}, u32[]{:S(2)}, u32[]{:S(2)}) collective-permute-start(f32[8,256]{1,0:T(8,128)S(1)} %get-tuple-element.42), channel_id=1, source_target_pairs={{0,24},{4,28},{8,16},{12,20},{16,8},{20,12},{24,0},{28,4},{1,25},{... | collective-permute-start | bytes 24584 | tf_op jit(solution)/shard_map/ppermute | solution.py:433
  38.8 3.7 %collective-permute-start.11 = (f32[8,256]{1,0:T(8,128)S(1)}, f32[8,256]{1,0:T(8,128)S(1)}, u32[]{:S(2)}, u32[]{:S(2)}) collective-permute-start(f32[8,256]{1,0:T(8,128)S(1)} %get-tuple-element.43), channel_id=1, source_target_pairs={{0,16},{4,20},{8,24},{12,28},{16,0},{20,4},{24,8},{28,12},{1,17},{... | collective-permute-start | bytes 24584 | tf_op jit(solution)/shard_map/ppermute | solution.py:433
  39.4 3.7 %collective-permute-start.12 = (f32[8,256]{1,0:T(8,128)S(1)}, f32[8,256]{1,0:T(8,128)S(1)}, u32[]{:S(2)}, u32[]{:S(2)}) collective-permute-start(f32[8,256]{1,0:T(8,128)S(1)} %get-tuple-element.44), channel_id=1, source_target_pairs={{0,8},{4,12},{8,0},{12,4},{16,24},{20,28},{24,16},{28,20},{1,9},{5... | collective-permute-start | bytes 24584 | tf_op jit(solution)/shard_map/ppermute | solution.py:433
